TPU v7x, 256 devices: a whole 4x4x8 slice. The times are simulated.
256 devices in a mesh: dom: 32 (over x, z), feat: 8 (over y, core).
Axes of the slice: x: 4, y: 4, z: 8, core: 2. Of those that a mesh axis runs over, the one named last changes fastest.
Arguments:
- node_feats: bfloat16 [131072, 256], P(('dom', 'feat')), may hold values from -6 to 6
- w_query: bfloat16 [256, 256], replicated, may hold values from -0.375 to 0.375
- w_key: bfloat16 [256, 256], replicated, may hold values from -0.375 to 0.375
- w_value: bfloat16 [256, 256], replicated, may hold values from -0.375 to 0.375
- w_graph: bfloat16 [256, 256], replicated, may hold values from -0.375 to 0.375
- adj_tiles: bfloat16 [12288, 128, 128], P(('dom', 'feat')), may hold values from -0.15625 to 0.15625
- tile_rows: int32 [12288], P(('dom', 'feat')), may hold values from 0 to 4, as said below
- tile_cols: int32 [12288], P(('dom', 'feat')), may hold values from 0 to 47
- send_lists: int32 [32, 2, 8], P('dom'), may hold values from 0 to 31
- cotangent: bfloat16 [131072, 256], P(('dom', 'feat')), may hold values from -6 to 6
Outputs:
- layer_out: bfloat16 [131072, 256], P(('dom', 'feat'))
- grad_feats: bfloat16 [131072, 256], P(('dom', 'feat'))
- grad_query: float32 [256, 256], replicated
- grad_key: float32 [256, 256], replicated
- grad_value: float32 [256, 256], replicated
- grad_graph: float32 [256, 256], replicated
Inputs may be any that keep to these rules, and one draw needn't show every extreme that they name: `tile_rows`: A slot holding 4 is empty; on each device the live slots come first, 12 to 48 of them, and some device has all 48 live. `send_lists`: blocks may repeat within a list.
All inputs are finite; a program needn't handle non-finite values.
Results may differ from a plain program's by a relative error of at most 0.0047.
The roundings to bfloat16 on the way count: a program that leaves them out, or rounds other values in their place, can miss the bound.
Values may be sent and summed in bfloat16 or wider, within the bound.
A program may use at most 128 MiB of HBM per device.

v0:
```python
import jax
import jax.numpy as jnp
from jax import lax
from jax.sharding import PartitionSpec as P

HEADS = 8
HEAD_DIM = 32


def passed_along(value, axis, steps):
    count = lax.axis_size(axis)
    initial, last = (max(0, -steps), min(count, count - steps))
    return lax.ppermute(value, axis, [(source, source + steps) for source in range(initial, last)])


def feature_map(values):
    return jnp.where(values > 0, values + 1.0, jnp.exp(jnp.minimum(values, 0.0)))


def feature_slope(values):
    return jnp.where(values > 0, 1.0, jnp.exp(jnp.minimum(values, 0.0)))


def rounded(values):
    return lax.optimization_barrier(values.astype(jnp.bfloat16)).astype(jnp.float32)


def shards(
    node_feats,
    w_query,
    w_key,
    w_value,
    w_graph,
    adj_tiles,
    tile_rows,
    tile_cols,
    send_lists,
    cotangent,
):
    precise = lax.Precision.HIGHEST
    node_rows, width = node_feats.shape
    tile_count, tile_size = (adj_tiles.shape[0], adj_tiles.shape[1])
    local_blocks = node_rows // tile_size
    feat_size = lax.axis_size("feat")
    part_blocks = local_blocks * feat_size
    rim_blocks = send_lists.shape[2]
    ext_count = part_blocks + 2 * rim_blocks
    head_count, head_width = (HEADS, HEAD_DIM)
    shape_heads = (node_rows, head_count, head_width)
    weights_all = jnp.concatenate([w_query, w_key, w_value, w_graph], 1)
    projected = jnp.dot(node_feats, weights_all, preferred_element_type=jnp.float32)
    query_proj = projected[:, :width]
    key_proj = projected[:, width : 2 * width]
    value_proj = projected[:, 2 * width : 3 * width]
    k_feat = feature_map(key_proj).astype(jnp.bfloat16)
    v_feat = value_proj.astype(jnp.bfloat16)
    prop_in = projected[:, 3 * width :].astype(jnp.bfloat16)
    partition = lax.all_gather(prop_in, "feat", axis=0, tiled=True).reshape(
        part_blocks, tile_size, width
    )
    send_rows = send_lists[0]
    from_lower = passed_along(partition[send_rows[1]], "dom", 1)
    from_upper = passed_along(partition[send_rows[0]], "dom", -1)
    extended = jnp.concatenate([partition, from_lower, from_upper], 0)
    rounds = tile_count // tile_count
    tiles_grouped = adj_tiles.reshape(rounds, tile_count, tile_size, tile_size)
    rows_grouped = tile_rows.reshape(rounds, tile_count)
    cols_grouped = tile_cols.reshape(rounds, tile_count)
    block_ids = jnp.arange(local_blocks)[None, :]

    def forward_round(running, inputs):
        tile_group, row_group, col_group = inputs
        product = jnp.einsum(
            "tij,tjd->tid", tile_group, extended[col_group], preferred_element_type=jnp.float32
        )
        onehot = (row_group[:, None] == block_ids).astype(jnp.float32)
        return (running + jnp.einsum("tr,tid->rid", onehot, product, precision=precise), None)

    prop_blocks, _ = lax.scan(
        forward_round,
        jnp.zeros((local_blocks, tile_size, width), jnp.float32),
        (tiles_grouped, rows_grouped, cols_grouped),
    )
    prop = prop_blocks.reshape(node_rows, width)
    k_heads_low = k_feat.reshape(shape_heads)
    state_part = jnp.einsum(
        "nhi,nhj->hij", k_heads_low, v_feat.reshape(shape_heads), preferred_element_type=jnp.float32
    )
    keysum_part = jnp.sum(k_feat.astype(jnp.float32).reshape(shape_heads), axis=0)
    kv_state, key_sum = lax.psum((state_part, keysum_part), ("dom", "feat"))
    q_heads = rounded(feature_map(query_proj)).reshape(shape_heads)
    k_heads = k_feat.astype(jnp.float32).reshape(shape_heads)
    v_heads = v_feat.astype(jnp.float32).reshape(shape_heads)
    numerator = jnp.einsum("nhi,hij->nhj", q_heads, kv_state, precision=precise)
    denominator = jnp.einsum("nhi,hi->nh", q_heads, key_sum, precision=precise)
    attn = numerator / denominator[:, :, None]
    layer_out = (0.5 * attn.reshape(node_rows, width) + 0.5 * prop).astype(jnp.bfloat16)
    grad_half = cotangent.astype(jnp.float32) * 0.5
    grad_heads = grad_half.reshape(shape_heads)
    d_numer = grad_heads / denominator[:, :, None]
    d_denom = -jnp.sum(grad_heads * attn, axis=-1) / denominator
    d_qfeat = (
        jnp.einsum("nhj,hij->nhi", d_numer, kv_state, precision=precise)
        + d_denom[:, :, None] * key_sum[None]
    )
    state_grad_part = jnp.einsum("nhi,nhj->hij", q_heads, d_numer, precision=precise)
    keysum_grad_part = jnp.einsum("nh,nhi->hi", d_denom, q_heads, precision=precise)
    d_state, d_keysum = lax.psum((state_grad_part, keysum_grad_part), ("dom", "feat"))
    d_kfeat = jnp.einsum("nhj,hij->nhi", v_heads, d_state, precision=precise) + d_keysum[None]
    d_value = jnp.einsum("nhi,hij->nhj", k_heads, d_state, precision=precise).reshape(
        node_rows, width
    )
    d_query = d_qfeat.reshape(node_rows, width) * feature_slope(query_proj)
    d_key = d_kfeat.reshape(node_rows, width) * feature_slope(key_proj)
    grad_blocks = grad_half.astype(jnp.bfloat16).reshape(local_blocks, tile_size, width)
    padded_rows = jnp.concatenate([grad_blocks, jnp.zeros((1, tile_size, width), jnp.bfloat16)], 0)

    def backward_round(running, inputs):
        tile_group, row_group, col_group = inputs
        product = jnp.einsum(
            "tij,tid->tjd", tile_group, padded_rows[row_group], preferred_element_type=jnp.float32
        )
        return (running + jax.ops.segment_sum(product, col_group, num_segments=ext_count), None)

    ext_grads, _ = lax.scan(
        backward_round,
        jnp.zeros((ext_count, tile_size, width), jnp.float32),
        (tiles_grouped, rows_grouped, cols_grouped),
    )
    own_grads = ext_grads[:part_blocks]
    lower_back = ext_grads[part_blocks : part_blocks + rim_blocks]
    upper_back = ext_grads[part_blocks + rim_blocks :]
    incoming = jnp.zeros((part_blocks, tile_size, width), jnp.float32)
    from_above = passed_along(lower_back, "dom", -1)
    from_below = passed_along(upper_back, "dom", 1)
    incoming = incoming.at[send_rows[1]].add(from_above).at[send_rows[0]].add(from_below)
    prop_grad = lax.psum_scatter(
        (own_grads + incoming).reshape(part_blocks * tile_size, width),
        "feat",
        scatter_dimension=0,
        tiled=True,
    )
    grads_all = jnp.concatenate([d_query, d_key, d_value, prop_grad], 1)
    grad_feats = lax.dot_general(
        grads_all, weights_all.astype(jnp.float32), (((1,), (1,)), ((), ())), precision=precise
    ).astype(jnp.bfloat16)
    local_terms = lax.dot_general(
        node_feats,
        grads_all,
        (((0,), (0,)), ((), ())),
        precision=precise,
        preferred_element_type=jnp.float32,
    )
    summed = lax.psum(local_terms, ("dom", "feat"))
    grad_query = summed[:, :width]
    grad_key = summed[:, width : 2 * width]
    grad_value = summed[:, 2 * width : 3 * width]
    grad_graph = summed[:, 3 * width :]
    return (layer_out, grad_feats, grad_query, grad_key, grad_value, grad_graph)


def solution(mesh):
    return jax.shard_map(
        shards,
        mesh=mesh,
        in_specs=(
            P(("dom", "feat"), None),
            P(),
            P(),
            P(),
            P(),
            P(("dom", "feat"), None, None),
            P(("dom", "feat")),
            P(("dom", "feat")),
            P("dom", None, None),
            P(("dom", "feat"), None),
        ),
        out_specs=(P(("dom", "feat"), None), P(("dom", "feat"), None), P(), P(), P(), P()),
        check_vma=False,
    )
```

profile of v0, /device:TPU:1, one launch (start us, length us, event | category | flops | bytes accessed | tf_op | source)
XLA Modules:
  0.0 571.6 jit_solution(16092185890895304619)
XLA Ops:
  7.2 0.0 copy-start
  7.2 0.0 all-gather.2.cloned.1.call-start
  7.2 1.1 constant_dynamic-update-slice_fusion.3
  8.3 0.9 constant_dynamic-update-slice_fusion.2
  9.2 0.9 constant_dynamic-update-slice_fusion.1
  10.1 0.9 constant_dynamic-update-slice_fusion
  11.1 3.0 fusion.22
  14.1 0.7 fusion.21
  14.8 0.0 all-gather.2.cloned.1.call-update
  14.8 0.0 reduce-scatter.2.cloned.1.call-start
  14.9 0.1 convert_multiply_fusion
  15.0 2.5 gather_fusion.3
  17.5 5.6 convolution_bitcast_fusion
  23.1 6.6 %copy.35 = f32[48,128,256]{2,1,0:T(8,128)} copy(f32[48,128,256]{1,2,0:T(8,128)} %convolution_bitcast_fusion) | data formatting | bytes 12582912 | tf_op jit(solution)/shard_map/while/body/eval_jaxpr/tij,tid->tjd/dot_general | solution.py:120
  29.6 3.4 broadcast.77
  33.0 14.8 %scatter_fusion = f32[48,128,256]{2,1,0:T(8,128)} fusion(f32[48,128,256]{2,1,0:T(8,128)} %broadcast.77, s32[48]{0:T(128)S(1)} %copy-done.13, f32[48,128,256]{2,1,0:T(8,128)} %copy.35), kind=kCustom, calls=%fused_computation.4 | custom fusion | flops 1572864 | bytes 18874560 | tf_op jit(solution)/shard_map/while/body/eval_jaxpr/scatter-add | solution.py:123
  47.9 2.7 fusion.19
  50.6 1.3 collective-permute-start.2
  51.9 6.0 %collective-permute-start.3 = (f32[8,128,256]{2,1,0:T(8,128)}, f32[8,128,256]{2,1,0:T(8,128)}, u32[]{:S(2)}, u32[]{:S(2)}) collective-permute-start(f32[8,128,256]{2,1,0:T(8,128)} %get-tuple-element.66), channel_id=1, source_target_pairs={{0,8},{8,16},{16,24},{24,32},{32,40},{40,48},{48,56},{56,64},{64,7... | collective-permute-start | bytes 3145736 | tf_op jit(solution)/shard_map/ppermute | solution.py:13
  57.9 4.6 slice.70
  62.5 13.4 %collective-permute-done.2 = f32[8,128,256]{2,1,0:T(8,128)} collective-permute-done((f32[8,128,256]{2,1,0:T(8,128)S(1)}, f32[8,128,256]{2,1,0:T(8,128)}, u32[]{:S(2)}, u32[]{:S(2)}) %collective-permute-start.2) | collective-permute-done | bytes 1048608 | tf_op jit(solution)/shard_map/ppermute | solution.py:13
  75.9 3.7 scatter_fusion.1
  79.6 3.6 scatter_fusion.2
  83.2 5.6 copy.49
  88.8 0.0 reduce-scatter.2.cloned.1.call-update
  88.8 0.0 all-reduce.5.cloned.1.call-start
  88.9 0.2 copy.32
  89.1 2.4 select_convert_fusion
  91.5 0.1 reduce_sum.21
  91.6 0.2 fusion.23
  91.8 85.0 %all-reduce.2 = (f32[8,32,32]{2,1,0:T(8,128)S(1)}, f32[8,32]{1,0:T(8,128)S(1)}) all-reduce(f32[8,32,32]{2,1,0:T(8,128)S(1)} %fusion.23, f32[8,32]{1,0:T(8,128)S(1)} %reduce_sum.21), channel_id=1, replica_groups=mesh['dom'=32,'feat'=8] {'dom','feat'}, use_global_device_ids=true, to_apply=%region_0.1 | all-reduce | flops 8448 | bytes 67584 | tf_op jit(solution)/shard_map/psum | solution.py:90
  176.7 0.2 fusion.24
  177.0 1.3 multiply_reduce_fusion
  178.3 1.2 copy.31
  179.5 0.3 fusion.10
  179.8 1.1 fusion.8
  180.9 73.9 %all-reduce.1 = (f32[8,32,32]{2,1,0:T(8,128)S(1)}, f32[8,32]{1,0:T(8,128)S(1)}) all-reduce(f32[8,32,32]{2,1,0:T(8,128)} %fusion.8, f32[8,32]{1,0:T(8,128)S(1)} %bitcast.109), channel_id=1, replica_groups=mesh['dom'=32,'feat'=8] {'dom','feat'}, use_global_device_ids=true, to_apply=%region_4.5 | all-reduce | flops 8448 | bytes 67584 | tf_op jit(solution)/shard_map/psum | solution.py:108
  254.8 0.4 convolution_add_fusion
  255.2 2.5 fusion.3
  257.7 4.1 copy.50
  261.8 3.0 gather_fusion.1
  264.8 3.0 gather_fusion
  267.7 3.0 collective-permute-start
  270.8 1.5 collective-permute-start.1
  272.2 1.2 fusion.26
  273.5 2.6 bitcast_multiply_fusion.1
  276.0 5.6 collective-permute-done
  281.6 3.7 collective-permute-done.1
  285.4 1.9 pad_maximum_fusion
  287.3 4.4 gather_fusion.2
  291.6 5.6 fusion.25
  297.2 6.7 %copy.44 = f32[48,256,128]{1,0,2:T(8,128)} copy(f32[48,256,128]{2,1,0:T(8,128)} %fusion.25) | data formatting | bytes 12582912 | tf_op jit(solution)/shard_map/while/body/eval_jaxpr/tij,tjd->tid/dot_general | solution.py:73
  304.0 3.3 convolution_bitcast_fusion.2
  307.3 0.0 all-reduce.5.cloned.1.call-update
  307.3 5.0 fusion
  312.3 0.1 copy.30
  312.4 0.8 fusion.7
  313.2 2.5 fusion.5
  315.8 244.7 %all-reduce.5.cloned.1.call-done = f32[256,1024]{0,1:T(8,128)} async-done(((f32[256,1024]{0,1:T(8,128)}), f32[256,1024]{0,1:T(8,128)}) %all-reduce.5.cloned.1.call-update) | async-done | bytes 1048592 | tf_op jit(solution)/shard_map/psum | solution.py:154
  560.5 1.3 fusion.20
  561.7 0.8 copy.40
  562.6 0.8 copy.39
  563.4 0.8 copy.38
  564.2 0.8 copy.37
  (46 shorter events, 0.1 us)
Async XLA Ops:
  7.2 10.3 %copy-start = (bf16[48,128,128]{2,1,0:T(8,128)(2,1)S(1)}, bf16[48,128,128]{2,1,0:T(8,128)(2,1)}, u32[]{:S(2)}) copy-start(bf16[48,128,128]{2,1,0:T(8,128)(2,1)} %param.15) | copy-start | bytes 4718596
  7.2 7.7 %copy-start.10 = (bf16[512,256]{1,0:T(8,128)(2,1)S(1)}, bf16[512,256]{1,0:T(8,128)(2,1)}, u32[]{:S(2)}) copy-start(bf16[512,256]{1,0:T(8,128)(2,1)} %param.19) | copy-start | bytes 786436
  7.2 250.5 %all-gather.2.cloned.1.call-start = ((), (), s32[]{:S(2)}) async-start(), calls=%async_computation.1 | async-start | bytes 2359296 | tf_op jit(solution)/shard_map/all_gather | solution.py:58
  11.1 3.7 copy-start.2
  11.1 3.9 copy-start.14
  14.8 289.1 %reduce-scatter.2.cloned.1.call-start = ((), (), s32[]{:S(2)}) async-start(), calls=%async_computation.2 | async-start | bytes 4718592 | tf_op jit(solution)/shard_map/reduce_scatter | solution.py:137
  29.6 3.4 copy-start.13
  50.6 25.3 %collective-permute-start.2 = (f32[8,128,256]{2,1,0:T(8,128)S(1)}, f32[8,128,256]{2,1,0:T(8,128)}, u32[]{:S(2)}, u32[]{:S(2)}) collective-permute-start(f32[8,128,256]{2,1,0:T(8,128)S(1)} %get-tuple-element.67), channel_id=1, source_target_pairs={{8,0},{16,8},{24,16},{32,24},{40,32},{48,40},{56,48},{64,56},{72,6... | collective-permute-start | bytes 3145736 | tf_op jit(solution)/shard_map/ppermute | solution.py:13
  51.9 10.6 %copy-start.12 = (s32[1,2,8]{2,1,0:T(2,128)S(1)}, s32[1,2,8]{2,1,0:T(2,128)}, u32[]{:S(2)}) copy-start(s32[1,2,8]{2,1,0:T(2,128)} %param.18) | copy-start | bytes 196
  51.9 27.7 %collective-permute-start.3 = (f32[8,128,256]{2,1,0:T(8,128)}, f32[8,128,256]{2,1,0:T(8,128)}, u32[]{:S(2)}, u32[]{:S(2)}) collective-permute-start(f32[8,128,256]{2,1,0:T(8,128)} %get-tuple-element.66), channel_id=1, source_target_pairs={{0,8},{8,16},{16,24},{24,32},{32,40},{40,48},{48,56},{56,64},{64,7... | collective-permute-start | bytes 3145736 | tf_op jit(solution)/shard_map/ppermute | solution.py:13
  88.8 471.6 %all-reduce.5.cloned.1.call-start = ((), (), s32[]{:S(2)}) async-start(), calls=%async_computation.3 | async-start | bytes 2097152 | tf_op jit(solution)/shard_map/psum | solution.py:154
  89.1 90.7 %copy-start.5 = (f32[512,256]{0,1:T(8,128)}, f32[512,256]{0,1:T(8,128)S(1)}, u32[]{:S(2)}) copy-start(f32[512,256]{0,1:T(8,128)S(1)} %copy.32) | copy-start | bytes 1572868
  176.7 1.5 copy-start.16
  257.7 15.8 %copy-start.8 = (pred[512,256]{0,1:T(8,128)(4,1)S(1)}, pred[512,256]{0,1:T(8,128)(4,1)}, u32[]{:S(2)}) copy-start(pred[512,256]{0,1:T(8,128)(4,1)} %get-tuple-element.62) | copy-start | bytes 393220
  257.7 15.8 %copy-start.9 = (pred[512,256]{0,1:T(8,128)(4,1)S(1)}, pred[512,256]{0,1:T(8,128)(4,1)}, u32[]{:S(2)}) copy-start(pred[512,256]{0,1:T(8,128)(4,1)} %get-tuple-element.72) | copy-start | bytes 393220
  267.7 17.6 %copy-start.1 = (bf16[4096,256]{1,0:T(8,128)(2,1)S(1)}, bf16[4096,256]{1,0:T(8,128)(2,1)}, u32[]{:S(2)}) copy-start(bf16[4096,256]{1,0:T(8,128)(2,1)} %copy.50) | copy-start | bytes 6291460
  267.7 13.9 %collective-permute-start = (bf16[8,128,256]{2,1,0:T(8,128)(2,1)}, bf16[8,128,256]{2,1,0:T(8,128)(2,1)S(1)}, u32[]{:S(2)}, u32[]{:S(2)}) collective-permute-start(bf16[8,128,256]{2,1,0:T(8,128)(2,1)} %gather_fusion), channel_id=1, source_target_pairs={{0,8},{8,16},{16,24},{24,32},{32,40},{40,48},{48,56},{56,64},{64,7... | collective-permute-start | bytes 1572872 | tf_op jit(solution)/shard_map/ppermute | solution.py:13
  270.8 14.6 %collective-permute-start.1 = (bf16[8,128,256]{2,1,0:T(8,128)(2,1)}, bf16[8,128,256]{2,1,0:T(8,128)(2,1)S(1)}, u32[]{:S(2)}, u32[]{:S(2)}) collective-permute-start(bf16[8,128,256]{2,1,0:T(8,128)(2,1)} %gather_fusion.1), channel_id=1, source_target_pairs={{8,0},{16,8},{24,16},{32,24},{40,32},{48,40},{56,48},{64,56},{72,6... | collective-permute-start | bytes 1572872 | tf_op jit(solution)/shard_map/ppermute | solution.py:13
  297.2 6.8 %copy-start.4 = (f32[8,32,512]{2,1,0:T(8,128)S(1)}, f32[8,32,512]{2,1,0:T(8,128)}, u32[]{:S(2)}) copy-start(f32[8,32,512]{2,1,0:T(8,128)} %fusion.26) | copy-start | bytes 1572868
  297.2 6.8 %copy-start.6 = (f32[512,256]{0,1:T(8,128)S(1)}, f32[512,256]{0,1:T(8,128)}, u32[]{:S(2)}) copy-start(f32[512,256]{0,1:T(8,128)} %get-tuple-element.68) | copy-start | bytes 1572868
  297.2 6.8 %copy-start.11 = (bf16[512,256]{1,0:T(8,128)(2,1)S(1)}, bf16[512,256]{1,0:T(8,128)(2,1)}, u32[]{:S(2)}) copy-start(bf16[512,256]{1,0:T(8,128)(2,1)} %param.10) | copy-start | bytes 786436
  307.3 5.9 %copy-start.3 = (bf16[256,1024]{1,0:T(8,128)(2,1)S(1)}, bf16[256,1024]{1,0:T(8,128)(2,1)}, u32[]{:S(2)}) copy-start(bf16[256,1024]{1,0:T(8,128)(2,1)} %copy-done.2) | copy-start | bytes 1572868
  307.3 5.9 %copy-start.7 = (f32[512,256]{0,1:T(8,128)S(1)}, f32[512,256]{0,1:T(8,128)}, u32[]{:S(2)}) copy-start(f32[512,256]{0,1:T(8,128)} %get-tuple-element.69) | copy-start | bytes 1572868
  307.3 5.9 %copy-start.15 = (f32[512,256]{0,1:T(8,128)S(1)}, f32[512,256]{0,1:T(8,128)}, u32[]{:S(2)}) copy-start(f32[512,256]{0,1:T(8,128)} %reduce-scatter.2.cloned.1.call-done) | copy-start | bytes 1572868
Sparse Core Ops, SparseCore 0:
  14.9 31.9 all-gather.1
  89.0 44.4 reduce-scatter.1
  307.4 253.0 all-reduce.4
where the time goes:
time: 573 us; the launch traced here: 572 us
  waiting for transfers between devices  267 us (47%)
  blocking collectives  159 us (28%)
  local copies, waits for them, and re-layouts  57.4 us (10%)
  matrix products  32.1 us (6%)
  other arithmetic  29.9 us (5%)
  between operations  14 us (2%)
  starting transfers between devices  11.9 us (2%)
    psum x1, waiting for transfers between devices, shards(): summed = lax.psum(local_terms, ('dom', 'feat'))  245 us
    psum x1, blocking collectives, shards(): kv_state, key_sum = lax.psum((state_part, keysum_part), ('dom', 'feat'))  85 us
    psum x1, blocking collectives, shards(): lax.psum((state_grad_part, keysum_grad_part), ('dom', 'feat'))  73.9 us
    ppermute x4, waiting for transfers between devices, passed_along(): lax.ppermute(value, axis, [(source, source + steps) for source in range(i...  22.7 us
    scatter-add x1, other arithmetic, backward_round(): jax.ops.segment_sum(product, col_group, num_segments=ext_count)  14.8 us
    ppermute x4, starting transfers between devices, passed_along(): lax.ppermute(value, axis, [(source, source + steps) for source in range(i...  11.8 us
  transfers between devices with their start and end apart: 7, of which 4 were waited for; matrix products, arithmetic and copies ran while one was open for 18% of the time, Pallas kernels for 0%

commit v1 on v0

v1 whole, which is shorter than its diff:
```python
import functools

import jax
import jax.numpy as jnp
from jax import lax
from jax.experimental import pallas as pl
from jax.experimental.pallas import tpu as pltpu
from jax.sharding import PartitionSpec as P

HEADS = 8
HD = 32
MESH = pl.DeviceIdType.MESH
F32 = jnp.float32
BF16 = jnp.bfloat16
CORES = 2
LIMIT = 56 * 1024 * 1024

VM = pl.BlockSpec(memory_space=pltpu.VMEM)
SM = pl.BlockSpec(memory_space=pltpu.SMEM)
HB = pl.BlockSpec(memory_space=pl.ANY)


def dims(mesh_dom):
    zn = min(8, mesh_dom)
    return mesh_dom // zn, zn


def dot(a, b):
    return jnp.dot(a, b, preferred_element_type=F32)


def dot_tn(a, b):
    return lax.dot_general(a, b, (((0,), (0,)), ((), ())), preferred_element_type=F32)


def dot_nt(a, b):
    return lax.dot_general(a, b, (((1,), (1,)), ((), ())), preferred_element_type=F32)


def split(value, parts):
    out = []
    for _ in range(parts - 1):
        top = value.astype(BF16)
        out.append(top)
        value = value - top.astype(F32)
    out.append(value.astype(BF16))
    return out


def dots(op, a, b):
    terms = [op(p, q) for p in a for q in b]
    total = terms[-1]
    for term in terms[-2::-1]:
        total = total + term
    return total


def feature(z):
    return jnp.where(z > 0, z + 1.0, jnp.exp(jnp.minimum(z, 0.0)))


def slope(z):
    return jnp.where(z > 0, 1.0, jnp.exp(jnp.minimum(z, 0.0)))


def same_head(rows, cols):
    r = lax.broadcasted_iota(jnp.int32, (rows, cols), 0) // HD
    c = lax.broadcasted_iota(jnp.int32, (rows, cols), 1) // HD
    return r == c


def compact(full):
    lane = lax.broadcasted_iota(jnp.int32, (HD, full.shape[1]), 1) // HD
    out = jnp.zeros((HD, full.shape[1]), F32)
    for h in range(HEADS):
        out = out + jnp.where(lane == h, full[h * HD : (h + 1) * HD, :], 0.0)
    return out


def block_diag(small):
    width = small.shape[1]
    return jnp.where(same_head(width, width), jnp.concatenate([small] * HEADS, 0), 0.0)


def state_store(st_ref, small, row):
    for s in range(4):
        st_ref[s] = small[8 * s : 8 * s + 8]
    st_ref[4] = jnp.broadcast_to(row, (8, row.shape[1]))
    for s in range(5, 8):
        st_ref[s] = jnp.zeros((8, row.shape[1]), F32)


def state_load(st_ref):
    small = jnp.concatenate([st_ref[s] for s in range(4)], 0)
    return small, st_ref[4][0:1]


def first_kernel(
    rows, cols, x, wq, wk, wv, wg, adj, cot, qf, kf, vf, pin, st, pext, acc, g5
):
    tiles = adj.shape[0]
    blocks, size = g5.shape[0] - 1, g5.shape[1]
    xv = x[...]
    k = feature(dot(xv, wk[...])).astype(BF16)
    v = dot(xv, wv[...]).astype(BF16)
    kf[...] = k
    vf[...] = v
    state_store(st, compact(dot_tn(k, v)), jnp.sum(k.astype(F32), axis=0, keepdims=True))
    qf[...] = feature(dot(xv, wq[...])).astype(BF16)
    pin[...] = dot(xv, wg[...]).astype(BF16).reshape(pin.shape)
    for b in range(blocks):
        g5[b] = (cot[b * size : (b + 1) * size, :].astype(F32) * 0.5).astype(BF16)
    g5[blocks] = jnp.zeros(g5.shape[1:], BF16)

    def clear(c, carry):
        acc[c] = jnp.zeros(acc.shape[1:], F32)
        return carry

    lax.fori_loop(0, acc.shape[0], clear, 0)

    def one(t, carry):
        product = dot_tn(adj[t], g5[rows[t]])
        c = cols[t]
        acc[c] = acc[c] + product
        return carry

    lax.fori_loop(0, tiles, one, 0, unroll=4)

    def low(c, carry):
        pext[c] = acc[c].astype(BF16)
        return carry

    lax.fori_loop(0, acc.shape[0], low, 0)


def place(zn):
    d, f = lax.axis_index("dom"), lax.axis_index("feat")
    return d, f, d // zn, d % zn, f // CORES, f % CORES


def greet(peers):
    barrier = pltpu.get_barrier_semaphore()
    for peer in peers:
        pl.semaphore_signal(barrier, inc=1, device_id=peer, device_id_type=MESH)
    pl.semaphore_wait(barrier, len(peers))


def send(src, dst, ssem, rsem, dev):
    copy = pltpu.make_async_remote_copy(
        src_ref=src, dst_ref=dst, send_sem=ssem, recv_sem=rsem, device_id=dev, device_id_type=MESH
    )
    copy.start()
    return copy


def ring_peers(xn, zn, yn):
    d, f, x, z, y, c = place(zn)
    feat = [(d, (f + k) % (yn * CORES)) for k in range(1, yn * CORES)]
    zs = [(x * zn + (z + k) % zn, f) for k in range(1, zn)]
    xs = [((x + k) % xn * zn + z, f) for k in range(1, xn)]
    return feat, zs, xs


class Reduce:
    def __init__(self, xn, zn, yn, st, out, rsbuf, zbuf, xbuf, ssem, rsem):
        self.xn, self.zn, self.yn = xn, zn, yn
        self.st, self.out, self.rsbuf, self.zbuf, self.xbuf = st, out, rsbuf, zbuf, xbuf
        self.ssem, self.rsem = ssem, rsem
        self.used = 0
        self.sent = []
        self.d, self.f, self.x, self.z, self.y, self.c = place(zn)
        self.feat, self.zs, self.xs = ring_peers(xn, zn, yn)

    def spread(self, srcs, dst, peers):
        copies = []
        for src, peer in zip(srcs, peers):
            n = self.used
            self.used += 1
            copies.append(send(src, dst, self.ssem.at[n], self.rsem.at[n], peer))
        self.sent += copies
        return copies

    def scatter(self):
        n = len(self.feat) + 1
        self.pending = self.spread(
            [self.st.at[(self.f + k) % n] for k in range(1, n)], self.rsbuf.at[self.f], self.feat
        )
        self.rsbuf[self.f] = self.st[self.f]

    def total(self, buf):
        for copy in self.pending:
            copy.wait_recv()
        value = buf[0]
        for i in range(1, buf.shape[0]):
            value = value + buf[i]
        return value

    def along_z(self):
        self.zbuf[self.z] = self.total(self.rsbuf)
        self.pending = self.spread([self.zbuf.at[self.z]] * len(self.zs), self.zbuf.at[self.z], self.zs)

    def along_x(self):
        self.xbuf[self.x] = self.total(self.zbuf)
        self.pending = self.spread([self.xbuf.at[self.x]] * len(self.xs), self.xbuf.at[self.x], self.xs)

    def gather(self):
        self.out[self.f] = self.total(self.xbuf)
        self.pending = self.spread([self.out.at[self.f]] * len(self.feat), self.out.at[self.f], self.feat)

    def finish(self):
        for copy in self.pending:
            copy.wait_recv()
        for copy in self.sent:
            copy.wait_send()


def reduce_scratch(xn, zn, yn, width):
    count = 2 * (yn * CORES - 1) + zn - 1 + xn - 1
    return [
        pltpu.VMEM((8, 8, width), F32),
        pltpu.VMEM((zn, 8, width), F32),
        pltpu.VMEM((xn, 8, width), F32),
        pltpu.SemaphoreType.DMA((count,)),
        pltpu.SemaphoreType.DMA((count,)),
    ]


def second_kernel(
    xn, zn, yn,
    st, pin, pext,
    out, part, own, back,
    rsbuf, zbuf, xbuf, rs_s, rs_r,
    sib, rimsum, ag_s, ag_r, rb_s, rb_r,
):
    d, f, x, z, y, c = place(zn)
    dn = xn * zn
    feat, zs, xs = ring_peers(xn, zn, yn)
    sibling = (d, f + 1 - 2 * c)
    up_y = (d, (y + 1) % yn * CORES + c)
    down_y = (d, (y + yn - 1) % yn * CORES + c)
    above, below = ((d + 1) % dn, f), ((d + dn - 1) % dn, f)
    mine = pin.shape[0]
    half = mine // 2
    hrow = sib.shape[1]
    nown = own.shape[0]
    nrim = sib.shape[0] - nown
    greet(feat + zs + xs + [above, below])

    red = Reduce(xn, zn, yn, st, out, rsbuf, zbuf, xbuf, rs_s, rs_r)
    red.scatter()
    other = pl.ds(pl.multiple_of(hrow * (1 - c), hrow), hrow)
    keep = pl.ds(pl.multiple_of(hrow * c, hrow), hrow)
    sib_rim = send(
        pext.at[pl.ds(nown, nrim), other], sib.at[pl.ds(nown, nrim)], rb_s.at[0], rb_r.at[0], sibling
    )

    def chunk(dev_f, h, count=1):
        return part.at[pl.ds(dev_f * mine + h * half, half * count)]

    part[pl.ds(f * mine, mine)] = pin[...]
    a0 = send(chunk(f, 0), chunk(f, 0), ag_s.at[0], ag_r.at[0], up_y)
    b1 = send(chunk(f, 1), chunk(f, 1), ag_s.at[1], ag_r.at[1], down_y)
    a1 = send(chunk(f, 1), chunk(f, 1), ag_s.at[2], ag_r.at[2], up_y)
    b0 = send(chunk(f, 0), chunk(f, 0), ag_s.at[3], ag_r.at[3], down_y)
    s_own = send(chunk(f, 0, 2), chunk(f, 0, 2), ag_s.at[4], ag_r.at[4], sibling)
    sib_own = send(
        pext.at[pl.ds(0, nown), other], sib.at[pl.ds(0, nown)], rb_s.at[1], rb_r.at[1], sibling
    )

    red.along_z()

    sib_rim.wait_recv()

    def add_rim(i, carry):
        rimsum[i] = (pext[nown + i, keep].astype(F32) + sib[nown + i].astype(F32)).astype(BF16)
        return carry

    lax.fori_loop(0, nrim, add_rim, 0)
    nb = nrim // 2
    to_below = send(rimsum.at[pl.ds(0, nb)], back.at[0], rb_s.at[2], rb_r.at[2], below)
    to_above = send(rimsum.at[pl.ds(nb, nb)], back.at[1], rb_s.at[3], rb_r.at[3], above)

    fu = (y + 1) % yn * CORES + c
    fd = (y + yn - 1) % yn * CORES + c
    fo = (y + 2) % yn * CORES + c
    a0.wait_recv()
    fa = send(chunk(fd, 0), chunk(fd, 0), ag_s.at[5], ag_r.at[5], up_y)
    s0 = send(chunk(fd, 0), chunk(fd, 0), ag_s.at[7], ag_r.at[7], sibling)
    b1.wait_recv()
    fb = send(chunk(fu, 1), chunk(fu, 1), ag_s.at[6], ag_r.at[6], down_y)
    s1 = send(chunk(fu, 1), chunk(fu, 1), ag_s.at[8], ag_r.at[8], sibling)
    red.along_x()
    red.gather()

    sib_own.wait_recv()

    def add_own(i, carry):
        own[i] = pext[i, keep].astype(F32) + sib[i].astype(F32)
        return carry

    lax.fori_loop(0, nown, add_own, 0)

    a1.wait_recv()
    s2 = send(chunk(fd, 1), chunk(fd, 1), ag_s.at[9], ag_r.at[9], sibling)
    b0.wait_recv()
    s3 = send(chunk(fu, 0), chunk(fu, 0), ag_s.at[10], ag_r.at[10], sibling)
    fa.wait_recv()
    s4 = send(chunk(fo, 0), chunk(fo, 0), ag_s.at[11], ag_r.at[11], sibling)
    fb.wait_recv()
    s5 = send(chunk(fo, 1), chunk(fo, 1), ag_s.at[12], ag_r.at[12], sibling)
    for copy in (to_below, to_above, s_own, s0, s1, s2, s3, s4, s5):
        copy.wait_recv()

    @pl.when(d == dn - 1)
    def _():
        back[0] = jnp.zeros(back.shape[1:], BF16)

    @pl.when(d == 0)
    def _():
        back[1] = jnp.zeros(back.shape[1:], BF16)

    red.finish()
    for copy in (sib_rim, sib_own, to_below, to_above, a0, b1, a1, b0, s_own, fa, fb, s0, s1, s2, s3, s4, s5):
        copy.wait_send()


def third_kernel(lists, st, qf, cot, x, wq, part, own, back, attn_o, dq_o, st2, own_o, picks, work):
    small, ks = state_load(st)
    width = ks.shape[1]
    kv = split(block_diag(small), 3)
    ks_col = jnp.broadcast_to(ks, (128, width)).T
    head = same_head(width, width)
    ks_bd = split(jnp.where(head, jnp.concatenate([ks_col] * (width // 128), 1), 0.0), 3)
    q = qf[...]
    den = dots(dot, [q], ks_bd)
    rden = 1.0 / den
    attn = dots(dot, [q], kv) * rden
    attn_o[...] = attn
    g = cot[...].astype(F32) * 0.5
    ones = jnp.where(head, 1.0, 0.0).astype(BF16)
    dden = -dots(dot, split(g * attn, 3), [ones]) * rden
    dqf = dots(dot_nt, [g.astype(BF16)], kv) * rden + dden * ks
    dq_o[...] = dqf * slope(dot(x[...], wq[...]))
    dstate = compact(dots(dot_tn, [q], split(g * rden, 3)))
    state_store(st2, dstate, jnp.sum(dden * q.astype(F32), axis=0, keepdims=True))

    nb = lists.shape[1]
    for i in range(own.shape[0]):
        work[i] = own[i]
    for s in range(nb):
        up, down = lists[1, s], lists[0, s]
        work[up] = work[up] + back[0, s].astype(F32)
        work[down] = work[down] + back[1, s].astype(F32)
        picks[0, s] = part[up]
        picks[1, s] = part[down]
    for i in range(own.shape[0]):
        own_o[i] = work[i].astype(BF16)


def fourth_kernel(
    xn, zn, yn,
    st, own, picks,
    out, rim, pg,
    rsbuf, zbuf, xbuf, rs_s, rs_r,
    ybuf, ysum, res, y_s, y_r, f_s, f_r,
):
    d, f, x, z, y, c = place(zn)
    dn = xn * zn
    feat, zs, xs = ring_peers(xn, zn, yn)
    sibling = (d, f + 1 - 2 * c)
    yu, yd, yo = (y + 1) % yn, (y + yn - 1) % yn, (y + 2) % yn
    up_y, down_y = (d, yu * CORES + c), (d, yd * CORES + c)
    above, below = ((d + 1) % dn, f), ((d + dn - 1) % dn, f)
    per = own.shape[0] // yn
    hb = per // 2
    hrow = own.shape[1]
    greet(feat + zs + xs + [above, below])

    red = Reduce(xn, zn, yn, st, out, rsbuf, zbuf, xbuf, rs_s, rs_r)
    red.scatter()

    def piece(yy, h):
        return own.at[pl.ds(yy * per + h * hb, hb)]

    keep = pl.ds(pl.multiple_of(hrow * c, hrow), hrow)
    y0 = send(piece(yo, 0), ybuf.at[0], y_s.at[0], y_r.at[0], up_y)
    y1 = send(piece(yo, 1), ybuf.at[1], y_s.at[1], y_r.at[1], down_y)
    y2 = send(piece(yu, 1), ybuf.at[2], y_s.at[2], y_r.at[2], up_y)
    y3 = send(piece(yd, 0), ybuf.at[3], y_s.at[3], y_r.at[3], down_y)
    to_above = send(picks.at[0, :, keep], rim.at[0, :, keep], f_s.at[0], f_r.at[0], above)
    to_below = send(picks.at[1, :, keep], rim.at[1, :, keep], f_s.at[1], f_r.at[1], below)

    red.along_z()

    y0.wait_recv()

    def add0(i, carry):
        ysum[0, i] = (own[yu * per + i].astype(F32) + ybuf[0, i].astype(F32)).astype(BF16)
        return carry

    lax.fori_loop(0, hb, add0, 0)
    y4 = send(ysum.at[0], ybuf.at[4], y_s.at[4], y_r.at[4], up_y)
    y1.wait_recv()

    def add1(i, carry):
        ysum[1, i] = (own[yd * per + hb + i].astype(F32) + ybuf[1, i].astype(F32)).astype(BF16)
        return carry

    lax.fori_loop(0, hb, add1, 0)
    y5 = send(ysum.at[1], ybuf.at[5], y_s.at[5], y_r.at[5], down_y)
    red.along_x()
    red.gather()

    to_above.wait_recv()
    s0 = send(rim.at[0, :, keep], rim.at[0, :, keep], f_s.at[2], f_r.at[2], sibling)
    to_below.wait_recv()
    s1 = send(rim.at[1, :, keep], rim.at[1, :, keep], f_s.at[3], f_r.at[3], sibling)

    for copy in (y2, y3, y4, y5):
        copy.wait_recv()

    def last(i, carry):
        base = y * per
        res[i] = own[base + i].astype(F32) + ybuf[4, i].astype(F32) + ybuf[3, i].astype(F32)
        res[hb + i] = own[base + hb + i].astype(F32) + ybuf[2, i].astype(F32) + ybuf[5, i].astype(F32)
        return carry

    lax.fori_loop(0, hb, last, 0)
    pg_copy = send(res.at[pl.ds(hb * (1 - c), hb)], pg.at[:, keep], y_s.at[6], y_r.at[6], sibling)
    pg[:, keep] = res[pl.ds(hb * c, hb)]
    pg_copy.wait_recv()
    s0.wait_recv()
    s1.wait_recv()
    for copy in (s0, s1, pg_copy, to_above, to_below, y0, y1, y2, y3, y4, y5):
        copy.wait_send()

    @pl.when(d == 0)
    def _():
        rim[0] = jnp.zeros(rim.shape[1:], BF16)

    @pl.when(d == dn - 1)
    def _():
        rim[1] = jnp.zeros(rim.shape[1:], BF16)

    red.finish()


def fifth_kernel(
    rows, cols, x, wq, wk, wv, wg, kf, vf, attn, dq, st, part, rim, adj, pg,
    layer, gfeat, local,
    ext, acc, sems,
):
    nown = part.shape[0]
    nb = rim.shape[1]
    copies = [
        pltpu.make_async_copy(part, ext.at[pl.ds(0, nown)], sems.at[0]),
        pltpu.make_async_copy(rim.at[0], ext.at[pl.ds(nown, nb)], sems.at[1]),
        pltpu.make_async_copy(rim.at[1], ext.at[pl.ds(nown + nb, nb)], sems.at[2]),
    ]
    for copy in copies:
        copy.start()
    small, dks = state_load(st)
    ds = split(block_diag(small), 2)
    xv = x[...]
    v = vf[...]
    dk = (dots(dot_nt, [v], ds) + dks) * slope(dot(xv, wk[...]))
    dv = dots(dot, [kf[...]], ds)
    pgv = pg[...].reshape(xv.shape)
    total = None
    for i, (grad, w) in enumerate(((dq[...], wq), (dk, wk), (dv, wv), (pgv, wg))):
        parts = split(grad, 2)
        local[i] = dots(dot_tn, [xv], parts)
        term = dots(dot_nt, parts, [w[...]])
        total = term if total is None else total + term
    gfeat[...] = total.astype(BF16)
    for copy in copies:
        copy.wait()
    acc[...] = jnp.zeros(acc.shape, F32)

    def one(t, carry):
        r = rows[t]
        acc[r] = acc[r] + dot(adj[t], ext[cols[t]])
        return carry

    lax.fori_loop(0, adj.shape[0], one, 0, unroll=4)
    size = acc.shape[1]
    for b in range(acc.shape[0] - 1):
        here = slice(b * size, (b + 1) * size)
        layer[here, :] = (0.5 * attn[here, :] + 0.5 * acc[b]).astype(BF16)


def sixth_kernel(xn, zn, yn, local, out, sbuf, ybuf, h1, h2, xbuf, h3, zbuf, s_s, s_r):
    d, f, x, z, y, c = place(zn)
    sibling = (d, f + 1 - 2 * c)
    ys = [(d, (y + k) % yn * CORES + c) for k in range(1, yn)]
    _, zs, xs = ring_peers(xn, zn, yn)
    greet([sibling] + ys + zs + xs)
    nm = local.shape[0]
    hrow = sbuf.shape[1]
    yrow = hrow // yn
    xrow = yrow // xn
    used = [0]
    sent = []

    def go(src, dst, dev):
        n = used[0]
        used[0] += 1
        copy = send(src, dst, s_s.at[n], s_r.at[n], dev)
        sent.append(copy)
        return copy

    def rows_of(start, count):
        return pl.ds(pl.multiple_of(start, count), count)

    first = go(local.at[:, rows_of(hrow * (1 - c), hrow)], sbuf, sibling)
    first.wait_recv()

    def add1(m, carry):
        h1[m] = local[m, rows_of(hrow * c, hrow)] + sbuf[m]
        return carry

    lax.fori_loop(0, nm, add1, 0)
    copies = [
        go(h1.at[:, rows_of((y + k) % yn * yrow, yrow)], ybuf.at[k - 1], ys[k - 1]) for k in range(1, yn)
    ]
    for copy in copies:
        copy.wait_recv()

    def add2(m, carry):
        value = h1[m, rows_of(y * yrow, yrow)]
        for k in range(1, yn):
            value = value + ybuf[k - 1, m]
        h2[m] = value
        return carry

    lax.fori_loop(0, nm, add2, 0)
    copies = [
        go(h2.at[:, rows_of((x + k) % xn * xrow, xrow)], xbuf.at[k - 1], xs[k - 1]) for k in range(1, xn)
    ]
    for copy in copies:
        copy.wait_recv()
    lanes = h2.shape[2] // 128
    units = h3.shape[0]
    for m in range(nm):
        value = h2[m, rows_of(x * xrow, xrow)]
        for k in range(1, xn):
            value = value + xbuf[k - 1, m]
        for r in range(xrow // 8):
            for a in range(lanes):
                h3[(m * (xrow // 8) + r) * lanes + a] = value[r * 8 : r * 8 + 8, a * 128 : a * 128 + 128]
    uz = units // zn
    copies = [
        go(h3.at[pl.ds((z + k) % zn * uz, uz)], zbuf.at[k - 1], zs[k - 1]) for k in range(1, zn)
    ]
    for copy in copies:
        copy.wait_recv()
    value = h3[pl.ds(z * uz, uz)]
    for k in range(1, zn):
        value = value + zbuf[k - 1]
    here = out.at[c, y, x, pl.ds(z * uz, uz)]
    out[c, y, x, pl.ds(z * uz, uz)] = value
    for copy in [go(here, here, peer) for peer in zs]:
        copy.wait_recv()
    for copy in [go(out.at[c, y, x], out.at[c, y, x], peer) for peer in xs]:
        copy.wait_recv()
    for copy in [go(out.at[c, y], out.at[c, y], peer) for peer in ys]:
        copy.wait_recv()
    go(out.at[c], out.at[c], sibling).wait_recv()
    for copy in sent:
        copy.wait_send()


def seventh_kernel(out, g0, g1, g2, g3):
    cn, yn, xn, units = out.shape[:4]
    grads = (g0, g1, g2, g3)
    lanes = g0.shape[1] // 128
    per = units // len(grads) // lanes
    for c in range(cn):
        for y in range(yn):
            for x in range(xn):
                for m, ref in enumerate(grads):
                    for r in range(per):
                        row = (((c * yn + y) * xn + x) * per + r) * 8
                        for a in range(lanes):
                            ref[row : row + 8, a * 128 : a * 128 + 128] = out[c, y, x, (m * per + r) * lanes + a]


def plain(limit=LIMIT):
    return pltpu.CompilerParams(vmem_limit_bytes=limit)


def linked(number, limit=LIMIT):
    return pltpu.CompilerParams(collective_id=number, has_side_effects=True, vmem_limit_bytes=limit)


def shards(xn, zn, x, wq, wk, wv, wg, adj, rows, cols, lists, cot):
    yn = lax.axis_size("feat") // CORES
    n, w = x.shape
    tiles, size = adj.shape[0], adj.shape[1]
    local_blocks = n // size
    nown = local_blocks * yn * CORES
    nb = lists.shape[2]
    next_ = nown + 2 * nb
    lists = lists.reshape(lists.shape[1:])
    S = jax.ShapeDtypeStruct
    half = size // 2

    qf, kf, vf, pin, st, pext = pl.pallas_call(
        first_kernel,
        out_shape=[
            S((n, w), BF16), S((n, w), BF16), S((n, w), BF16), S((local_blocks, size, w), BF16),
            S((8, 8, w), F32), S((next_, size, w), BF16),
        ],
        in_specs=[SM, SM] + [VM] * 7,
        out_specs=[VM] * 6,
        scratch_shapes=[pltpu.VMEM((next_, size, w), F32), pltpu.VMEM((local_blocks + 1, size, w), BF16)],
        compiler_params=plain(),
        name="first",
    )(rows, cols, x, wq, wk, wv, wg, adj, cot)

    st, part, own, back = pl.pallas_call(
        functools.partial(second_kernel, xn, zn, yn),
        out_shape=[
            S((8, 8, w), F32), S((nown, size, w), BF16), S((nown, half, w), F32), S((2, nb, half, w), BF16),
        ],
        in_specs=[VM] * 3,
        out_specs=[VM] * 4,
        scratch_shapes=reduce_scratch(xn, zn, yn, w) + [
            pltpu.VMEM((next_, half, w), BF16),
            pltpu.VMEM((2 * nb, half, w), BF16),
            pltpu.SemaphoreType.DMA((13,)),
            pltpu.SemaphoreType.DMA((13,)),
            pltpu.SemaphoreType.DMA((4,)),
            pltpu.SemaphoreType.DMA((4,)),
        ],
        compiler_params=linked(0),
        name="second",
    )(st, pin, pext)

    attn, dq, st2, own, picks = pl.pallas_call(
        third_kernel,
        out_shape=[
            S((n, w), F32), S((n, w), F32), S((8, 8, w), F32), S((nown, half, w), BF16),
            S((2, nb, size, w), BF16),
        ],
        in_specs=[SM] + [VM] * 8,
        out_specs=[VM] * 5,
        scratch_shapes=[pltpu.VMEM((nown, half, w), F32)],
        compiler_params=plain(),
        name="third",
    )(lists, st, qf, cot, x, wq, part, own, back)

    st2, rim, pg = pl.pallas_call(
        functools.partial(fourth_kernel, xn, zn, yn),
        out_shape=[S((8, 8, w), F32), S((2, nb, size, w), BF16), S((local_blocks, size, w), F32)],
        in_specs=[VM] * 3,
        out_specs=[VM] * 3,
        scratch_shapes=reduce_scratch(xn, zn, yn, w) + [
            pltpu.VMEM((6, local_blocks, half, w), BF16),
            pltpu.VMEM((2, local_blocks, half, w), BF16),
            pltpu.VMEM((2 * local_blocks, half, w), F32),
            pltpu.SemaphoreType.DMA((7,)),
            pltpu.SemaphoreType.DMA((7,)),
            pltpu.SemaphoreType.DMA((4,)),
            pltpu.SemaphoreType.DMA((4,)),
        ],
        compiler_params=linked(1),
        name="fourth",
    )(st2, own, picks)

    layer, gfeat, local = pl.pallas_call(
        fifth_kernel,
        out_shape=[S((n, w), BF16), S((n, w), BF16), S((4, w, w), F32)],
        in_specs=[SM, SM] + [VM] * 10 + [HB, HB] + [VM] * 2,
        out_specs=[VM] * 3,
        scratch_shapes=[
            pltpu.VMEM((next_, size, w), BF16),
            pltpu.VMEM((local_blocks + 1, size, w), F32),
            pltpu.SemaphoreType.DMA((3,)),
        ],
        compiler_params=plain(),
        name="fifth",
    )(rows, cols, x, wq, wk, wv, wg, kf, vf, attn, dq, st2, part, rim, adj, pg)

    yrow = w // CORES // yn
    xrow = yrow // xn
    units = 4 * (xrow // 8) * (w // 128)
    count = 2 * (1 + yn - 1 + xn - 1 + zn - 1)
    out = pl.pallas_call(
        functools.partial(sixth_kernel, xn, zn, yn),
        out_shape=S((CORES, yn, xn, units, 8, 128), F32),
        in_specs=[VM],
        out_specs=VM,
        scratch_shapes=[
            pltpu.VMEM((4, w // CORES, w), F32),
            pltpu.VMEM((yn - 1, 4, yrow, w), F32),
            pltpu.VMEM((4, w // CORES, w), F32),
            pltpu.VMEM((4, yrow, w), F32),
            pltpu.VMEM((max(xn - 1, 1), 4, xrow, w), F32),
            pltpu.VMEM((units, 8, 128), F32),
            pltpu.VMEM((max(zn - 1, 1), units // zn, 8, 128), F32),
            pltpu.SemaphoreType.DMA((count,)),
            pltpu.SemaphoreType.DMA((count,)),
        ],
        compiler_params=linked(2),
        name="sixth",
    )(local)

    grads = pl.pallas_call(
        seventh_kernel,
        out_shape=[S((w, w), F32)] * 4,
        in_specs=[VM],
        out_specs=[VM] * 4,
        compiler_params=plain(),
        name="seventh",
    )(out)
    return (layer, gfeat, *grads)


def solution(mesh):
    xn, zn = dims(mesh.shape["dom"])
    return jax.shard_map(
        functools.partial(shards, xn, zn),
        mesh=mesh,
        in_specs=(
            P(("dom", "feat"), None),
            P(),
            P(),
            P(),
            P(),
            P(("dom", "feat"), None, None),
            P(("dom", "feat")),
            P(("dom", "feat")),
            P("dom", None, None),
            P(("dom", "feat"), None),
        ),
        out_specs=(P(("dom", "feat"), None), P(("dom", "feat"), None), P(), P(), P(), P()),
        check_vma=False,
    )
```

time: 573 us -> 124 us (0.22)
  waiting for transfers between devices: 267 us -> 0 us
  blocking collectives: 159 us -> 0 us
  Pallas kernels: 0 us -> 123 us
  local copies, waits for them, and re-layouts: 57.4 us -> 0 us
  matrix products: 32.1 us -> 0 us
  other arithmetic: 29.9 us -> 0 us
  between operations: 14 us -> 0.66 us
  starting transfers between devices: 11.9 us -> 0 us
    psum x1 -> x0, waiting for transfers between devices: 245 us -> none  [shards(): summed = lax.psum(local_terms, ('dom', 'feat'))]
    psum x2 -> x0, blocking collectives: 159 us -> none  [the longest x1 85 us: shards(): kv_state, key_sum = lax.psum((state_part, keysum_part), ('dom', 'feat'))]
    pallas_call x0 -> x7, Pallas kernels: none -> 123 us  [the longest x1 41.9 us: shards(): pl.pallas_call(functools.partial(sixth_kernel, xn, zn, yn), out_shape=S((...]
    dot_general x14 -> x0, matrix products: 32.1 us -> none  [the longest x1 5.57 us: forward_round(): jnp.einsum('tij,tjd->tid', tile_group, extended[col_group], preferred_ele...]
    ppermute x4 -> x0, waiting for transfers between devices: 22.7 us -> none  [passed_along(): lax.ppermute(value, axis, [(source, source + steps) for source in range(i...]
    scatter-add x3 -> x0, other arithmetic: 22.2 us -> none  [the longest x1 14.8 us: backward_round(): jax.ops.segment_sum(product, col_group, num_segments=ext_count)]
    dot_general x4 -> x0, local copies, waits for them, and re-layouts: 13.4 us -> none  [the longest x1 6.74 us: forward_round(): jnp.einsum('tij,tjd->tid', tile_group, extended[col_group], preferred_ele...]
    gather x4 -> x0, local copies, waits for them, and re-layouts: 12.8 us -> none  [the longest x1 4.37 us: forward_round(): extended[col_group]]
  transfers between devices with their start and end apart: 7 -> 0, of which waited for: 4 -> 0; matrix products, arithmetic and copies ran while one was open for 18% -> 0% of each run, Pallas kernels for 0% -> 0%
where the time goes in v1:
time: 124 us
  Pallas kernels  123 us (99%)
    pallas_call x1, Pallas kernels, shards(): pl.pallas_call(functools.partial(sixth_kernel, xn, zn, yn), out_shape=S((...  41.9 us
    pallas_call x1, Pallas kernels, shards(): pl.pallas_call(functools.partial(second_kernel, xn, zn, yn), out_shape=[S...  33.3 us
    pallas_call x1, Pallas kernels, shards(): pl.pallas_call(functools.partial(fourth_kernel, xn, zn, yn), out_shape=[S...  23.5 us
    pallas_call x1, Pallas kernels, shards(): pl.pallas_call(first_kernel, out_shape=[S((n, w), BF16), S((n, w), BF16),...  8.71 us
    pallas_call x1, Pallas kernels, shards(): pl.pallas_call(fifth_kernel, out_shape=[S((n, w), BF16), S((n, w), BF16),...  7.92 us
    pallas_call x1, Pallas kernels, shards(): pl.pallas_call(third_kernel, out_shape=[S((n, w), F32), S((n, w), F32), S...  5.74 us

profile of v1, /device:TPU:1, one launch (start us, length us, event | category | flops | bytes accessed | tf_op | source)
XLA Modules:
  0.0 124.0 jit_solution(1639096305238162819)
XLA Ops:
  0.6 8.7 %first.1 = (bf16[512,256]{1,0:T(8,128)(2,1)}, bf16[512,256]{1,0:T(8,128)(2,1)}, bf16[512,256]{1,0:T(8,128)(2,1)}, bf16[4,128,256]{2,1,0:T(8,128)(2,1)}, f32[8,8,...) custom-call(s32[48]{0:T(128)} %rows.3, s32[48]{0:T(128)} %cols.3, bf16[512,256]{1,0:T(8,128)(2,1)} %x.5, bf16[256,256]{1,0:T(8,128)(2,1)} %wq.5, ...), custom_call_target="tpu_custom_call" | custom-call | tf_op jit(solution)/shard_map/first/pallas_call | solution.py:608
  9.3 33.3 %second.1 = (f32[8,8,256]{2,1,0:T(8,128)}, bf16[32,128,256]{2,1,0:T(8,128)(2,1)}, f32[32,64,256]{2,1,0:T(8,128)}, bf16[2,8,64,256]{3,2,1,0:T(8,128)(2,1)}) custom-call(f32[8,8,256]{2,1,0:T(8,128)} %get-tuple-element.33.st, bf16[4,128,256]{2,1,0:T(8,128)(2,1)} %get-tuple-element.34.pin, bf16[48,128,256]{2,1,0:T(8,128)(2,1)} %get-tuple-element.35.pext), custom_call_target="tpu_custom_call" | custom-call | tf_op jit(solution)/shard_map/second/pallas_call | solution.py:621
  42.6 5.7 %third.1 = (f32[512,256]{1,0:T(8,128)}, f32[512,256]{1,0:T(8,128)}, f32[8,8,256]{2,1,0:T(8,128)}, bf16[32,64,256]{2,1,0:T(8,128)(2,1)}, bf16[2,8,128,256]{3,2,1,0:T(8,128)(2,1)}) custom-call(s32[2,8]{1,0:T(2,128)} %bitcast.1, f32[8,8,256]{2,1,0:T(8,128)} %get-tuple-element.36.st, bf16[512,256]{1,0:T(8,128)(2,1)} %get-tuple-element.37.qf, ...), custom_call_target="tpu_custom_call" | custom-call | tf_op jit(solution)/shard_map/third/pallas_call | solution.py:640
  48.4 23.5 %fourth.1 = (f32[8,8,256]{2,1,0:T(8,128)}, bf16[2,8,128,256]{3,2,1,0:T(8,128)(2,1)}, f32[4,128,256]{2,1,0:T(8,128)}) custom-call(f32[8,8,256]{2,1,0:T(8,128)} %get-tuple-element.43.st, bf16[32,64,256]{2,1,0:T(8,128)(2,1)} %get-tuple-element.44.own, bf16[2,8,128,256]{3,2,1,0:T(8,128)(2,1)} %get-tuple-element.45.picks), custom_call_target="tpu_custom_call" | custom-call | tf_op jit(solution)/shard_map/fourth/pallas_call | solution.py:653
  71.9 7.9 %fifth.1 = (bf16[512,256]{1,0:T(8,128)(2,1)}, bf16[512,256]{1,0:T(8,128)(2,1)}, f32[4,256,256]{2,1,0:T(8,128)}) custom-call(s32[48]{0:T(128)} %rows.3, s32[48]{0:T(128)} %cols.3, bf16[512,256]{1,0:T(8,128)(2,1)} %x.5, bf16[256,256]{1,0:T(8,128)(2,1)} %wq.5, bf16[256,256]{1,0:T(8,128)(2,1)} %wk.3, bf16[256,256]{1,0:T(8,128)(2,1)} %wv.3, bf16[256,256]{1,0:T(8,128)(2,1)} %wg.3, ...), custom_call_target="tpu_custom_call" | custom-call | tf_op jit(solution)/shard_map/fifth/pallas_call | solution.py:671
  79.8 41.9 %sixth.1.out = f32[2,4,4,8,8,128]{5,4,3,2,1,0:T(8,128)} custom-call(f32[4,256,256]{2,1,0:T(8,128)} %get-tuple-element.51.local), custom_call_target="tpu_custom_call" | custom-call | tf_op jit(solution)/shard_map/sixth/pallas_call | solution.py:689
  121.8 2.2 %seventh.1 = (f32[256,256]{1,0:T(8,128)}, f32[256,256]{1,0:T(8,128)}, f32[256,256]{1,0:T(8,128)}, f32[256,256]{1,0:T(8,128)}) custom-call(f32[2,4,4,8,8,128]{5,4,3,2,1,0:T(8,128)} %sixth.1.out), custom_call_target="tpu_custom_call" | custom-call | tf_op jit(solution)/shard_map/seventh/pallas_call | solution.py:709

commit v2 on v0

v2 whole, which is shorter than its diff:
```python
import functools
from types import SimpleNamespace

import jax
import jax.numpy as jnp
from jax import lax
from jax.experimental import pallas as pl
from jax.experimental.pallas import tpu as pltpu
from jax.sharding import PartitionSpec as P

HEADS = 8
HD = 32
MESH = pl.DeviceIdType.MESH
F32 = jnp.float32
BF16 = jnp.bfloat16
CORES = 2
LIMIT = 56 * 1024 * 1024

VM = pl.BlockSpec(memory_space=pltpu.VMEM)
SM = pl.BlockSpec(memory_space=pltpu.SMEM)
HB = pl.BlockSpec(memory_space=pl.ANY)


def dims(mesh_dom):
    zn = min(8, mesh_dom)
    return mesh_dom // zn, zn


def dot(a, b):
    return jnp.dot(a, b, preferred_element_type=F32)


def dot_tn(a, b):
    return lax.dot_general(a, b, (((0,), (0,)), ((), ())), preferred_element_type=F32)


def dot_nt(a, b):
    return lax.dot_general(a, b, (((1,), (1,)), ((), ())), preferred_element_type=F32)


def split(value, parts):
    out = []
    for _ in range(parts - 1):
        top = value.astype(BF16)
        out.append(top)
        value = value - top.astype(F32)
    out.append(value.astype(BF16))
    return out


def dots(op, a, b):
    terms = [op(p, q) for p in a for q in b]
    total = terms[-1]
    for term in terms[-2::-1]:
        total = total + term
    return total


def feature(z):
    return jnp.where(z > 0, z + 1.0, jnp.exp(jnp.minimum(z, 0.0)))


def slope(z):
    return jnp.where(z > 0, 1.0, jnp.exp(jnp.minimum(z, 0.0)))


def same_head(rows, cols):
    r = lax.broadcasted_iota(jnp.int32, (rows, cols), 0) // HD
    c = lax.broadcasted_iota(jnp.int32, (rows, cols), 1) // HD
    return r == c


def compact(full):
    lane = lax.broadcasted_iota(jnp.int32, (HD, full.shape[1]), 1) // HD
    out = jnp.zeros((HD, full.shape[1]), F32)
    for h in range(HEADS):
        out = out + jnp.where(lane == h, full[h * HD : (h + 1) * HD, :], 0.0)
    return out


def block_diag(small):
    width = small.shape[1]
    return jnp.where(same_head(width, width), jnp.concatenate([small] * HEADS, 0), 0.0)


def state_store(st_ref, small, row):
    for s in range(4):
        st_ref[s] = small[8 * s : 8 * s + 8]
    st_ref[4] = jnp.broadcast_to(row, (8, row.shape[1]))
    for s in range(5, 8):
        st_ref[s] = jnp.zeros((8, row.shape[1]), F32)


def state_load(st_ref):
    small = jnp.concatenate([st_ref[s] for s in range(4)], 0)
    return small, st_ref[4][0:1]


def place(zn):
    d, f = lax.axis_index("dom"), lax.axis_index("feat")
    return d, f, d // zn, d % zn, f // CORES, f % CORES


def greet(peers):
    barrier = pltpu.get_barrier_semaphore()
    for peer in peers:
        pl.semaphore_signal(barrier, inc=1, device_id=peer, device_id_type=MESH)
    pl.semaphore_wait(barrier, len(peers))


def send(src, dst, ssem, rsem, dev):
    copy = pltpu.make_async_remote_copy(
        src_ref=src, dst_ref=dst, send_sem=ssem, recv_sem=rsem, device_id=dev, device_id_type=MESH
    )
    copy.start()
    return copy


def ring_peers(xn, zn, yn):
    d, f, x, z, y, c = place(zn)
    feat = [(d, (f + k) % (yn * CORES)) for k in range(1, yn * CORES)]
    zs = [(x * zn + (z + k) % zn, f) for k in range(1, zn)]
    xs = [((x + k) % xn * zn + z, f) for k in range(1, xn)]
    return feat, zs, xs


class Exchange:
    def __init__(self, xn, zn, yn, split_z, src, out, fbuf, zin, zbuf, xbuf, ssem, rsem):
        self.split_z = split_z
        self.src, self.out, self.fbuf, self.zin, self.zbuf, self.xbuf = src, out, fbuf, zin, zbuf, xbuf
        self.ssem, self.rsem = ssem, rsem
        self.used = 0
        self.sent = []
        self.pending = []
        self.xn, self.zn = xn, zn
        self.d, self.f, self.x, self.z, self.y, self.c = place(zn)
        self.feat, self.zs, self.xs = ring_peers(xn, zn, yn)

    def spread(self, srcs, dst, peers):
        copies = []
        for src, peer in zip(srcs, peers):
            n = self.used
            self.used += 1
            copies.append(send(src, dst, self.ssem.at[n], self.rsem.at[n], peer))
        self.sent += copies
        self.pending = copies

    def arrive(self):
        for copy in self.pending:
            copy.wait_recv()
        self.pending = []

    def total(self, buf):
        self.arrive()
        value = buf[0].astype(F32)
        for i in range(1, buf.shape[0]):
            value = value + buf[i].astype(F32)
        return value

    def scatter(self):
        n = len(self.feat) + 1
        self.spread([self.src.at[(self.f + k) % n] for k in range(1, n)], self.fbuf.at[self.f], self.feat)
        self.fbuf[self.f] = self.src[self.f]

    def along_z(self):
        value = self.total(self.fbuf)
        zn, z = self.zn, self.z
        if self.split_z:
            self.zin[...] = value.reshape(self.zin.shape)
            self.zbuf[z] = self.zin[z]
            self.spread([self.zin.at[(z + k) % zn] for k in range(1, zn)], self.zbuf.at[z], self.zs)
        else:
            self.zbuf[z] = value
            self.spread([self.zbuf.at[z]] * len(self.zs), self.zbuf.at[z], self.zs)

    def along_x(self):
        self.xbuf[self.x] = self.total(self.zbuf)
        here = self.xbuf.at[self.x]
        self.spread([here] * len(self.xs), here, self.xs)

    def back_z(self):
        if self.split_z:
            self.zin_out[self.z] = self.total(self.xbuf)
            here = self.zin_out.at[self.z]
            self.spread([here] * len(self.zs), here, self.zs)

    def gather(self):
        if self.split_z:
            self.arrive()
            value = self.zin_out[...].reshape(self.out.shape[1:])
        else:
            value = self.total(self.xbuf)
        self.out[self.f] = value.astype(self.out.dtype)
        here = self.out.at[self.f]
        self.spread([here] * len(self.feat), here, self.feat)

    def finish(self):
        for copy in self.sent:
            copy.wait_send()


def links(xn, zn, yn):
    return 2 * (yn * CORES - 1) + 2 * (zn - 1) + xn - 1


def state_scratch(name, xn, zn, yn, w):
    count = links(xn, zn, yn)
    return [
        (name + "src", pltpu.VMEM((8, 8, w), F32)),
        (name + "f", pltpu.VMEM((8, 8, w), F32)),
        (name + "z", pltpu.VMEM((zn, 8, w), F32)),
        (name + "x", pltpu.VMEM((xn, 8, w), F32)),
        (name + "ss", pltpu.SemaphoreType.DMA((count,))),
        (name + "rs", pltpu.SemaphoreType.DMA((count,))),
    ]


def grad_scratch(name, xn, zn, yn, rows, w):
    count = links(xn, zn, yn)
    n = yn * CORES
    part = rows // n
    return [
        (name + "src", pltpu.VMEM((n, part, w), BF16)),
        (name + "f", pltpu.VMEM((n, part, w), BF16)),
        (name + "zi", pltpu.VMEM((zn, part // zn, w), F32)),
        (name + "zo", pltpu.VMEM((zn, part // zn, w), F32)),
        (name + "z", pltpu.VMEM((zn, part // zn, w), F32)),
        (name + "x", pltpu.VMEM((xn, part // zn, w), F32)),
        (name + "ss", pltpu.SemaphoreType.DMA((count,))),
        (name + "rs", pltpu.SemaphoreType.DMA((count,))),
    ]


def state_sum(name, xn, zn, yn, m, out):
    g = vars(m)
    return Exchange(
        xn, zn, yn, False, g[name + "src"], out, g[name + "f"], None, g[name + "z"], g[name + "x"],
        g[name + "ss"], g[name + "rs"],
    )


def grad_sum(name, xn, zn, yn, m, out):
    g = vars(m)
    red = Exchange(
        xn, zn, yn, True, g[name + "src"], out, g[name + "f"], g[name + "zi"], g[name + "z"], g[name + "x"],
        g[name + "ss"], g[name + "rs"],
    )
    red.zin_out = g[name + "zo"]
    return red


def put_slices(ref, index, value):
    per = ref.shape[1]
    count = value.shape[0] // per
    for s in range(count):
        ref[index * count + s] = value[s * per : (s + 1) * per].astype(ref.dtype)


def layer_kernel(names, xn, zn, yn, *refs):
    m = SimpleNamespace(**dict(zip(names, refs)))
    d, f, x, z, y, c = place(zn)
    dn = xn * zn
    feat, zs, xs = ring_peers(xn, zn, yn)
    sibling = (d, f + 1 - 2 * c)
    yu, yd, yo = (y + 1) % yn, (y + yn - 1) % yn, (y + 2) % yn
    up_y, down_y = (d, yu * CORES + c), (d, yd * CORES + c)
    above, below = ((d + 1) % dn, f), ((d + dn - 1) % dn, f)
    tiles, size = m.adjv.shape[0], m.adjv.shape[1]
    w = m.x.shape[1]
    blocks = m.x.shape[0] // size
    nown = blocks * yn * CORES
    nb = m.lists.shape[1]
    next_ = nown + 2 * nb
    half = size // 2
    hb = blocks // 2
    keep = pl.ds(pl.multiple_of(half * c, half), half)
    other = pl.ds(pl.multiple_of(half * (1 - c), half), half)
    singles = []

    def go(n, src, dst, dev):
        copy = send(src, dst, m.ss.at[n], m.rs.at[n], dev)
        singles.append(copy)
        return copy

    peers = feat + zs + xs + [above, below]
    barrier = pltpu.get_barrier_semaphore()
    for peer in peers:
        pl.semaphore_signal(barrier, inc=1, device_id=peer, device_id_type=MESH)
    fetch = pltpu.make_async_copy(m.adj, m.adjv, m.ls.at[0])
    fetch.start()

    xv = m.x[...]
    key_proj = dot(xv, m.wk[...])
    kf = feature(key_proj).astype(BF16)
    vf = dot(xv, m.wv[...]).astype(BF16)
    m.kf[...] = kf
    m.vf[...] = vf
    state_store(m.asrc, compact(dot_tn(kf, vf)), jnp.sum(kf.astype(F32), axis=0, keepdims=True))
    xblocks = xv.reshape(blocks, size, w)
    m.xo[pl.ds(f * blocks, blocks)] = xblocks

    pl.semaphore_wait(barrier, len(peers))

    red1 = state_sum("a", xn, zn, yn, m, m.ast)
    red2 = state_sum("b", xn, zn, yn, m, m.st2)
    sum1 = grad_sum("c", xn, zn, yn, m, m.g1)
    sum2 = grad_sum("e", xn, zn, yn, m, m.g2)
    red1.scatter()

    def chunk(yy, h, count=1):
        return m.xo.at[pl.ds((yy * CORES + c) * blocks + h * hb, hb * count)]

    a0 = go(0, chunk(y, 0), chunk(y, 0), up_y)
    b1 = go(1, chunk(y, 1), chunk(y, 1), down_y)
    a1 = go(2, chunk(y, 1), chunk(y, 1), up_y)
    b0 = go(3, chunk(y, 0), chunk(y, 0), down_y)
    s_own = go(4, chunk(y, 0, 2), chunk(y, 0, 2), sibling)

    m.qf[...] = feature(dot(xv, m.wq[...])).astype(BF16)
    zero = jnp.zeros((size, w), BF16)
    for b in range(blocks):
        m.g5[b] = (m.cot[b * size : (b + 1) * size, :].astype(F32) * 0.5).astype(BF16)
    m.g5[blocks] = zero
    tpad = -(-tiles // 8) * 8
    down = lax.broadcasted_iota(jnp.int32, (tpad, 128), 0)
    across = lax.broadcasted_iota(jnp.int32, (tpad, 128), 1)

    def chains(table):
        col = jnp.full((tpad, 128), -1, jnp.int32)
        row = jnp.full((1, 128), -2, jnp.int32)
        for t in range(tiles):
            col = jnp.where(down == t, table[t], col)
            row = jnp.where(across[0:1] == t, table[t], row)
        same = (col == row) & (down < across)
        before = jnp.max(jnp.where(same, down, -1), axis=0, keepdims=True)
        final = jnp.max(jnp.where(col == across, down, -1), axis=0, keepdims=True)
        return [jnp.where(v < 0, tiles, v) for v in (before, final)]

    order = chains(m.cols) + chains(m.rows)
    m.ordv[...] = jnp.concatenate(order + order, 0)
    index = pltpu.make_async_copy(m.ordv, m.ords, m.ls.at[1])
    index.start()
    index.wait()
    fetch.wait()

    m.prod[tiles] = jnp.zeros((size, w), F32)
    step = tiles // 4

    def back_one(t, carry):
        m.prod[t] = dot_tn(m.adjv[t], m.g5[m.rows[t]]) + m.prod[m.ords[0, t]]
        return carry

    def back_tiles(part):
        lax.fori_loop(part * step, (part + 1) * step, back_one, 0, unroll=4)

    back_tiles(0)
    back_tiles(1)
    red1.along_z()
    back_tiles(2)
    back_tiles(3)
    red1.along_x()

    def to_sibling(start, count):
        def one(i, carry):
            m.pext[start + i] = m.prod[m.ords[1, start + i], other].astype(BF16)
            return carry

        lax.fori_loop(0, count, one, 0)

    a0.wait_recv()
    fa = go(5, chunk(yd, 0), chunk(yd, 0), up_y)
    b1.wait_recv()
    fb = go(6, chunk(yu, 1), chunk(yu, 1), down_y)
    to_sibling(nown, 2 * nb)
    sib_rim = go(7, m.pext.at[pl.ds(nown, 2 * nb)], m.sib.at[pl.ds(nown, 2 * nb)], sibling)
    s0 = go(8, chunk(yd, 0), chunk(yd, 0), sibling)
    s1 = go(9, chunk(yu, 1), chunk(yu, 1), sibling)
    to_sibling(0, nown)
    sib_own = go(10, m.pext.at[pl.ds(0, nown)], m.sib.at[pl.ds(0, nown)], sibling)
    red1.gather()

    sib_rim.wait_recv()

    def add_rim(i, carry):
        here = nown + i
        m.rimsum[i] = (m.prod[m.ords[1, here], keep] + m.sib[here].astype(F32)).astype(BF16)
        return carry

    lax.fori_loop(0, 2 * nb, add_rim, 0)
    to_below = go(11, m.rimsum.at[pl.ds(0, nb)], m.back.at[0], below)
    to_above = go(12, m.rimsum.at[pl.ds(nb, nb)], m.back.at[1], above)

    a1.wait_recv()
    s2 = go(13, chunk(yd, 1), chunk(yd, 1), sibling)
    b0.wait_recv()
    s3 = go(14, chunk(yu, 0), chunk(yu, 0), sibling)

    red1.arrive()
    small, ks = state_load(m.ast)
    kv = split(block_diag(small), 3)
    ks_col = jnp.broadcast_to(ks, (128, w)).T
    head = same_head(w, w)
    ks_bd = split(jnp.where(head, jnp.concatenate([ks_col] * (w // 128), 1), 0.0), 3)
    q = m.qf[...]
    rden = 1.0 / dots(dot, [q], ks_bd)
    attn = dots(dot, [q], kv) * rden
    g = m.cot[...].astype(F32) * 0.5
    ones = jnp.where(head, 1.0, 0.0).astype(BF16)
    dden = -dots(dot, split(g * attn, 3), [ones]) * rden
    dstate = compact(dots(dot_tn, [q], split(g * rden, 3)))
    state_store(m.bsrc, dstate, jnp.sum(dden * q.astype(F32), axis=0, keepdims=True))
    red2.scatter()
    m.attn[...] = attn
    dqf = dots(dot_nt, [g.astype(BF16)], kv) * rden + dden * ks
    dq = dqf * slope(dot(m.x[...], m.wq[...]))
    m.dq[...] = dq

    fa.wait_recv()
    s4 = go(15, chunk(yo, 0), chunk(yo, 0), sibling)
    fb.wait_recv()
    s5 = go(16, chunk(yo, 1), chunk(yo, 1), sibling)

    xv = m.x[...]
    put_slices(m.csrc, 0, dots(dot_tn, [xv], split(dq, 2)))
    put_slices(m.csrc, 1, dot_tn(xv, m.kf[...]))
    red2.along_z()

    for copy in (s_own, s0, s1, s2, s3, s4, s5):
        copy.wait_recv()
    for s in range(nb):
        m.picks[0, s] = m.xo[m.lists[1, s], keep]
        m.picks[1, s] = m.xo[m.lists[0, s], keep]
    f_above = go(17, m.picks.at[0], m.xr.at[0, :, keep], above)
    f_below = go(18, m.picks.at[1], m.xr.at[1, :, keep], below)
    sum1.scatter()

    sib_own.wait_recv()
    to_below.wait_recv()
    to_above.wait_recv()

    @pl.when(d == dn - 1)
    def _():
        m.back[0] = jnp.zeros(m.back.shape[1:], BF16)

    @pl.when(d == 0)
    def _():
        m.back[1] = jnp.zeros(m.back.shape[1:], BF16)

    def place_rims(base):
        def one(i, carry):
            b = base + i
            value = m.prod[m.ords[1, b], keep] + m.sib[b].astype(F32)
            for s in range(nb):
                value = value + jnp.where(m.lists[1, s] == b, m.back[0, s].astype(F32), 0.0)
                value = value + jnp.where(m.lists[0, s] == b, m.back[1, s].astype(F32), 0.0)
            m.ysend[b] = value.astype(BF16)
            return carry

        lax.fori_loop(0, blocks, one, 0)

    per = 2 * blocks

    def piece(yy, h):
        return m.ysend.at[pl.ds(yy * per + h * blocks, blocks)]

    place_rims(yo * per)
    y0 = go(19, piece(yo, 0), m.ybuf.at[0], up_y)
    place_rims(yo * per + blocks)
    y1 = go(20, piece(yo, 1), m.ybuf.at[1], down_y)
    red2.along_x()
    place_rims(yu * per + blocks)
    y2 = go(21, piece(yu, 1), m.ybuf.at[2], up_y)
    place_rims(yd * per)
    y3 = go(22, piece(yd, 0), m.ybuf.at[3], down_y)
    place_rims(yu * per)
    place_rims(yd * per + blocks)
    red2.gather()
    sum1.along_z()

    def add_piece(n, base):
        def one(i, carry):
            m.ysum[n, i] = (m.ysend[base + i].astype(F32) + m.ybuf[n, i].astype(F32)).astype(BF16)
            return carry

        lax.fori_loop(0, blocks, one, 0)

    y0.wait_recv()
    add_piece(0, yu * per)
    y4 = go(23, m.ysum.at[0], m.ybuf.at[4], up_y)
    y1.wait_recv()
    add_piece(1, yd * per + blocks)
    y5 = go(24, m.ysum.at[1], m.ybuf.at[5], down_y)
    place_rims(y * per)
    place_rims(y * per + blocks)

    def project(value, start):
        here = pl.ds(start, blocks)
        m.xp[here] = value
        value = dot(value.reshape(blocks * size, w), m.wg[...])
        m.ext[here] = value.astype(BF16).reshape(blocks, size, w)

    def project_own(i, carry):
        project(m.xo[pl.ds(i * blocks, blocks)], i * blocks)
        return carry

    lax.fori_loop(0, nown // blocks, project_own, 0)
    f_above.wait_recv()
    f_below.wait_recv()

    @pl.when(d == 0)
    def _():
        m.xr[0, :, keep] = jnp.zeros((nb, half, w), BF16)

    @pl.when(d == dn - 1)
    def _():
        m.xr[1, :, keep] = jnp.zeros((nb, half, w), BF16)

    s6 = go(25, m.xr.at[0, :, keep], m.xr.at[0, :, keep], sibling)
    s7 = go(26, m.xr.at[1, :, keep], m.xr.at[1, :, keep], sibling)
    sum1.along_x()

    red2.arrive()
    small, dks = state_load(m.st2)
    ds = split(block_diag(small), 2)
    xv = m.x[...]
    dk = (dots(dot_nt, [m.vf[...]], ds) + dks) * slope(dot(xv, m.wk[...]))
    put_slices(m.esrc, 0, dots(dot_tn, [xv], split(dk, 2)))
    m.dk[...] = dk

    s6.wait_recv()
    s7.wait_recv()
    for side in range(2):
        for i in range(nb // blocks):
            project(m.xr[side, i * blocks : (i + 1) * blocks], nown + side * nb + i * blocks)
    m.fprod[tiles] = jnp.zeros((size, w), F32)
    m.xprod[tiles] = jnp.zeros((size, w), F32)

    def fore_one(t, carry):
        tile = m.adjv[t]
        b = m.cols[t]
        before = m.ords[2, t]
        m.fprod[t] = dot(tile, m.ext[b]) + m.fprod[before]
        m.xprod[t] = dot(tile, m.xp[b]) + m.xprod[before]
        return carry

    lax.fori_loop(0, tiles // 2, fore_one, 0, unroll=4)
    sum1.back_z()
    lax.fori_loop(tiles // 2, tiles, fore_one, 0, unroll=4)
    graph = None
    for b in range(blocks):
        here = slice(b * size, (b + 1) * size)
        term = dots(dot_tn, split(m.xprod[m.ords[3, b]], 2), [m.g5[b]])
        graph = term if graph is None else graph + term
    put_slices(m.esrc, 1, graph)
    sum2.scatter()
    sum1.gather()
    for b in range(blocks):
        here = slice(b * size, (b + 1) * size)
        m.layer[here, :] = (0.5 * m.attn[here, :] + 0.5 * m.fprod[m.ords[3, b]]).astype(BF16)

    for copy in (y2, y3, y4, y5):
        copy.wait_recv()

    def last(i, carry):
        base = y * per
        m.res[i] = m.ysend[base + i].astype(F32) + m.ybuf[4, i].astype(F32) + m.ybuf[3, i].astype(F32)
        m.res[blocks + i] = (
            m.ysend[base + blocks + i].astype(F32) + m.ybuf[2, i].astype(F32) + m.ybuf[5, i].astype(F32)
        )
        return carry

    lax.fori_loop(0, blocks, last, 0)
    pg_copy = go(27, m.res.at[pl.ds(blocks * (1 - c), blocks)], m.pg.at[:, keep], sibling)
    m.pg[:, keep] = m.res[pl.ds(blocks * c, blocks)]
    sum2.along_z()
    dv = dots(dot, [m.kf[...]], ds)
    total = None
    for grad, weight in ((m.dq[...], m.wq), (m.dk[...], m.wk), (dv, m.wv)):
        term = dots(dot_nt, split(grad, 2), [weight[...]])
        total = term if total is None else total + term
    sum2.along_x()
    pg_copy.wait_recv()
    total = total + dots(dot_nt, split(m.pg[...].reshape(blocks * size, w), 2), [m.wg[...]])
    m.gfeat[...] = total.astype(BF16)
    sum2.back_z()
    sum2.gather()
    sum1.arrive()
    sum2.arrive()
    for red in (red1, red2, sum1, sum2):
        red.finish()
    for copy in singles:
        copy.wait_send()


def last_kernel(layer_i, gfeat_i, c1, c2, st, layer, gfeat, gq, gk, gv, gg):
    layer[...] = layer_i[...]
    gfeat[...] = gfeat_i[...]
    n = gq.shape[0]

    def mat(ref, index):
        per = ref.shape[1]
        count = n // per
        return jnp.concatenate([ref[index * count + s].astype(F32) for s in range(count)], 0)

    gq[...] = mat(c1, 0)
    gk[...] = mat(c2, 0)
    gg[...] = mat(c2, 1)
    small, _ = state_load(st)
    ds = split(block_diag(small), 2)
    gv[...] = dots(dot, split(mat(c1, 1), 2), ds)


def shards(xn, zn, x, wq, wk, wv, wg, adj, rows, cols, lists, cot):
    yn = lax.axis_size("feat") // CORES
    n, w = x.shape
    tiles, size = adj.shape[0], adj.shape[1]
    blocks = n // size
    nown = blocks * yn * CORES
    nb = lists.shape[2]
    next_ = nown + 2 * nb
    lists = lists.reshape(lists.shape[1:])
    S = jax.ShapeDtypeStruct
    V = pltpu.VMEM
    half = size // 2
    part = 2 * w // (yn * CORES)
    singles = 28

    ins = [
        ("rows", SM), ("cols", SM), ("lists", SM), ("x", VM), ("wq", VM), ("wk", VM), ("wv", VM), ("wg", VM),
        ("cot", VM), ("adj", HB),
    ]
    outs = [
        ("layer", S((n, w), BF16)),
        ("gfeat", S((n, w), BF16)),
        ("g1", S((yn * CORES, part, w), BF16)),
        ("g2", S((yn * CORES, part, w), BF16)),
        ("st2", S((8, 8, w), F32)),
    ]
    scratch = [
        ("adjv", V((tiles, size, size), BF16)),
        ("kf", V((n, w), BF16)),
        ("vf", V((n, w), BF16)),
        ("qf", V((n, w), BF16)),
        ("g5", V((blocks + 1, size, w), BF16)),
        ("xo", V((nown, size, w), BF16)),
        ("xr", V((2, nb, size, w), BF16)),
        ("xp", V((next_, size, w), BF16)),
        ("ext", V((next_, size, w), BF16)),
        ("prod", V((tiles + 1, size, w), F32)),
        ("fprod", V((tiles + 1, size, w), F32)),
        ("xprod", V((tiles + 1, size, w), F32)),
        ("pext", V((next_, half, w), BF16)),
        ("sib", V((next_, half, w), BF16)),
        ("rimsum", V((2 * nb, half, w), BF16)),
        ("back", V((2, nb, half, w), BF16)),
        ("picks", V((2, nb, half, w), BF16)),
        ("ysend", V((nown, half, w), BF16)),
        ("ybuf", V((6, blocks, half, w), BF16)),
        ("ysum", V((2, blocks, half, w), BF16)),
        ("res", V((2 * blocks, half, w), F32)),
        ("pg", V((blocks, size, w), F32)),
        ("attn", V((n, w), F32)),
        ("dq", V((n, w), F32)),
        ("dk", V((n, w), F32)),
        ("ast", V((8, 8, w), F32)),
        ("ordv", V((8, 128), jnp.int32)),
        ("ords", pltpu.SMEM((8, 128), jnp.int32)),
        ("ls", pltpu.SemaphoreType.DMA((2,))),
        ("ss", pltpu.SemaphoreType.DMA((singles,))),
        ("rs", pltpu.SemaphoreType.DMA((singles,))),
    ]
    scratch += state_scratch("a", xn, zn, yn, w) + state_scratch("b", xn, zn, yn, w)
    scratch += grad_scratch("c", xn, zn, yn, 2 * w, w) + grad_scratch("e", xn, zn, yn, 2 * w, w)
    names = [name for name, _ in ins + outs + scratch]
    made = pl.pallas_call(
        functools.partial(layer_kernel, names, xn, zn, yn),
        out_shape=[shape for _, shape in outs],
        in_specs=[spec for _, spec in ins],
        out_specs=[VM] * len(outs),
        scratch_shapes=[shape for _, shape in scratch],
        compiler_params=pltpu.CompilerParams(
            collective_id=0, has_side_effects=True, vmem_limit_bytes=LIMIT
        ),
        name="layer",
    )(rows, cols, lists, x, wq, wk, wv, wg, cot, adj)

    return pl.pallas_call(
        last_kernel,
        out_shape=[S((n, w), BF16)] * 2 + [S((w, w), F32)] * 4,
        in_specs=[VM] * 5,
        out_specs=[VM] * 6,
        compiler_params=pltpu.CompilerParams(vmem_limit_bytes=LIMIT),
        name="last",
    )(*made)


def solution(mesh):
    xn, zn = dims(mesh.shape["dom"])
    return jax.shard_map(
        functools.partial(shards, xn, zn),
        mesh=mesh,
        in_specs=(
            P(("dom", "feat"), None),
            P(),
            P(),
            P(),
            P(),
            P(("dom", "feat"), None, None),
            P(("dom", "feat")),
            P(("dom", "feat")),
            P("dom", None, None),
            P(("dom", "feat"), None),
        ),
        out_specs=(P(("dom", "feat"), None), P(("dom", "feat"), None), P(), P(), P(), P()),
        check_vma=False,
    )
```

time: 573 us -> 84.4 us (0.15)
  waiting for transfers between devices: 267 us -> 0 us
  blocking collectives: 159 us -> 0 us
  Pallas kernels: 0 us -> 83.6 us
  local copies, waits for them, and re-layouts: 57.4 us -> 0 us
  matrix products: 32.1 us -> 0 us
  other arithmetic: 29.9 us -> 0 us
  between operations: 14 us -> 0.64 us
  starting transfers between devices: 11.9 us -> 0 us
    psum x1 -> x0, waiting for transfers between devices: 245 us -> none  [shards(): summed = lax.psum(local_terms, ('dom', 'feat'))]
    psum x2 -> x0, blocking collectives: 159 us -> none  [the longest x1 85 us: shards(): kv_state, key_sum = lax.psum((state_part, keysum_part), ('dom', 'feat'))]
    pallas_call x0 -> x2, Pallas kernels: none -> 83.6 us  [the longest x1 81.1 us: shards(): pl.pallas_call(functools.partial(layer_kernel, names, xn, zn, yn), out_sh...]
    dot_general x14 -> x0, matrix products: 32.1 us -> none  [the longest x1 5.57 us: forward_round(): jnp.einsum('tij,tjd->tid', tile_group, extended[col_group], preferred_ele...]
    ppermute x4 -> x0, waiting for transfers between devices: 22.7 us -> none  [passed_along(): lax.ppermute(value, axis, [(source, source + steps) for source in range(i...]
    scatter-add x3 -> x0, other arithmetic: 22.2 us -> none  [the longest x1 14.8 us: backward_round(): jax.ops.segment_sum(product, col_group, num_segments=ext_count)]
    dot_general x4 -> x0, local copies, waits for them, and re-layouts: 13.4 us -> none  [the longest x1 6.74 us: forward_round(): jnp.einsum('tij,tjd->tid', tile_group, extended[col_group], preferred_ele...]
    gather x4 -> x0, local copies, waits for them, and re-layouts: 12.8 us -> none  [the longest x1 4.37 us: forward_round(): extended[col_group]]
  transfers between devices with their start and end apart: 7 -> 0, of which waited for: 4 -> 0; matrix products, arithmetic and copies ran while one was open for 18% -> 0% of each run, Pallas kernels for 0% -> 0%
where the time goes in v2:
time: 84.4 us; the launch traced here: 84.3 us
  Pallas kernels  83.6 us (99%)
    pallas_call x1, Pallas kernels, shards(): pl.pallas_call(functools.partial(layer_kernel, names, xn, zn, yn), out_sh...  81.1 us
    pallas_call x1, Pallas kernels, shards(): pl.pallas_call(last_kernel, out_shape=[S((n, w), BF16)] * 2 + [S((w, w),...  2.58 us

profile of v2, /device:TPU:1, one launch (start us, length us, event | category | flops | bytes accessed | tf_op | source)
XLA Modules:
  0.0 84.3 jit_solution(3866405226271588791)
XLA Ops:
  0.6 81.1 %layer.1 = (bf16[512,256]{1,0:T(8,128)(2,1)}, bf16[512,256]{1,0:T(8,128)(2,1)}, bf16[8,64,256]{2,1,0:T(8,128)(2,1)}, bf16[8,64,256]{2,1,0:T(8,128)(2,1)}, f32[8,8,256]{2,1,0:T(8,128)}) custom-call(s32[48]{0:T(128)} %refs_0_.1, s32[48]{0:T(128)} %refs_1_.1, s32[2,8]{1,0:T(2,128)} %bitcast.1, bf16[512,256]{1,0:T(8,128)(2,1)} %refs_3_.1, ...), custom_call_target="tpu_custom_call" | custom-call | tf_op jit(solution)/shard_map/layer/pallas_call | solution.py:675
  81.7 2.6 %last.1 = (bf16[512,256]{1,0:T(8,128)(2,1)}, bf16[512,256]{1,0:T(8,128)(2,1)}, f32[256,256]{1,0:T(8,128)}, f32[256,256]{1,0:T(8,128)}, f32[256,256]{1,0:T(8,128)}, /*index=5*/f32[256,256]{1,0:T(8,128)}) custom-call(bf16[512,256]{1,0:T(8,128)(2,1)} %get-tuple-element.11.layer_i, bf16[512,256]{1,0:T(8,128)(2,1)} %get-tuple-element.12.gfeat_i, ...), custom_call_target="tpu_custom_call" | custom-call | tf_op jit(solution)/shard_map/last/pallas_call | solution.py:687

commit v3 on v2

--- a/solution.py
+++ b/solution.py
@@ -125,16 +125,14 @@
 
 
 class Exchange:
-    def __init__(self, xn, zn, yn, split_z, src, out, fbuf, zin, zbuf, xbuf, ssem, rsem):
-        self.split_z = split_z
-        self.src, self.out, self.fbuf, self.zin, self.zbuf, self.xbuf = src, out, fbuf, zin, zbuf, xbuf
+    def __init__(self, group, me, src, out, fbuf, others, ssem, rsem):
+        self.group, self.me = group, me
+        self.src, self.out, self.fbuf, self.others = src, out, fbuf, others
         self.ssem, self.rsem = ssem, rsem
         self.used = 0
         self.sent = []
         self.pending = []
-        self.xn, self.zn = xn, zn
-        self.d, self.f, self.x, self.z, self.y, self.c = place(zn)
-        self.feat, self.zs, self.xs = ring_peers(xn, zn, yn)
+        self.last = fbuf
 
     def spread(self, srcs, dst, peers):
         copies = []
@@ -150,61 +148,47 @@
             copy.wait_recv()
         self.pending = []
 
-    def total(self, buf):
+    def total(self):
         self.arrive()
-        value = buf[0].astype(F32)
-        for i in range(1, buf.shape[0]):
-            value = value + buf[i].astype(F32)
+        value = self.last[0].astype(F32)
+        for i in range(1, self.last.shape[0]):
+            value = value + self.last[i].astype(F32)
         return value
 
     def scatter(self):
-        n = len(self.feat) + 1
-        self.spread([self.src.at[(self.f + k) % n] for k in range(1, n)], self.fbuf.at[self.f], self.feat)
-        self.fbuf[self.f] = self.src[self.f]
-
-    def along_z(self):
-        value = self.total(self.fbuf)
-        zn, z = self.zn, self.z
-        if self.split_z:
-            self.zin[...] = value.reshape(self.zin.shape)
-            self.zbuf[z] = self.zin[z]
-            self.spread([self.zin.at[(z + k) % zn] for k in range(1, zn)], self.zbuf.at[z], self.zs)
-        else:
-            self.zbuf[z] = value
-            self.spread([self.zbuf.at[z]] * len(self.zs), self.zbuf.at[z], self.zs)
-
-    def along_x(self):
-        self.xbuf[self.x] = self.total(self.zbuf)
-        here = self.xbuf.at[self.x]
-        self.spread([here] * len(self.xs), here, self.xs)
-
-    def back_z(self):
-        if self.split_z:
-            self.zin_out[self.z] = self.total(self.xbuf)
-            here = self.zin_out.at[self.z]
-            self.spread([here] * len(self.zs), here, self.zs)
+        self.spread([self.src.at[index] for index, _ in self.group], self.fbuf.at[self.me], [p for _, p in self.group])
+        self.fbuf[self.me] = self.src[self.me]
+
+    def along(self, n):
+        buf, peers, me = self.others[n]
+        buf[me] = self.total()
+        self.last = buf
+        self.spread([buf.at[me]] * len(peers), buf.at[me], peers)
 
     def gather(self):
-        if self.split_z:
-            self.arrive()
-            value = self.zin_out[...].reshape(self.out.shape[1:])
-        else:
-            value = self.total(self.xbuf)
-        self.out[self.f] = value.astype(self.out.dtype)
-        here = self.out.at[self.f]
-        self.spread([here] * len(self.feat), here, self.feat)
+        self.out[self.me] = self.total().astype(self.out.dtype)
+        here = self.out.at[self.me]
+        self.spread([here] * len(self.group), here, [p for _, p in self.group])
 
     def finish(self):
         for copy in self.sent:
             copy.wait_send()
 
 
-def links(xn, zn, yn):
-    return 2 * (yn * CORES - 1) + 2 * (zn - 1) + xn - 1
+def plane_group(xn, zn, yn):
+    d, f, x, z, y, c = place(zn)
+    n = yn * CORES
+    group = []
+    for i in range(xn):
+        for k in range(n):
+            if i or k:
+                px, pf = (x + i) % xn, (f + k) % n
+                group.append((px * n + pf, (px * zn + z, pf)))
+    return group, x * n + f
 
 
 def state_scratch(name, xn, zn, yn, w):
-    count = links(xn, zn, yn)
+    count = 2 * (yn * CORES - 1) + zn - 1 + xn - 1
     return [
         (name + "src", pltpu.VMEM((8, 8, w), F32)),
         (name + "f", pltpu.VMEM((8, 8, w), F32)),
@@ -216,16 +200,13 @@
 
 
 def grad_scratch(name, xn, zn, yn, rows, w):
-    count = links(xn, zn, yn)
-    n = yn * CORES
+    n = yn * CORES * xn
+    count = 2 * (n - 1) + zn - 1
     part = rows // n
     return [
         (name + "src", pltpu.VMEM((n, part, w), BF16)),
         (name + "f", pltpu.VMEM((n, part, w), BF16)),
-        (name + "zi", pltpu.VMEM((zn, part // zn, w), F32)),
-        (name + "zo", pltpu.VMEM((zn, part // zn, w), F32)),
-        (name + "z", pltpu.VMEM((zn, part // zn, w), F32)),
-        (name + "x", pltpu.VMEM((xn, part // zn, w), F32)),
+        (name + "z", pltpu.VMEM((zn, part, w), F32)),
         (name + "ss", pltpu.SemaphoreType.DMA((count,))),
         (name + "rs", pltpu.SemaphoreType.DMA((count,))),
     ]
@@ -233,20 +214,21 @@
 
 def state_sum(name, xn, zn, yn, m, out):
     g = vars(m)
-    return Exchange(
-        xn, zn, yn, False, g[name + "src"], out, g[name + "f"], None, g[name + "z"], g[name + "x"],
-        g[name + "ss"], g[name + "rs"],
-    )
+    d, f, x, z, y, c = place(zn)
+    feat, zs, xs = ring_peers(xn, zn, yn)
+    n = len(feat) + 1
+    group = [((f + k) % n, feat[k - 1]) for k in range(1, n)]
+    others = [(g[name + "z"], zs, z), (g[name + "x"], xs, x)]
+    return Exchange(group, f, g[name + "src"], out, g[name + "f"], others, g[name + "ss"], g[name + "rs"])
 
 
 def grad_sum(name, xn, zn, yn, m, out):
     g = vars(m)
-    red = Exchange(
-        xn, zn, yn, True, g[name + "src"], out, g[name + "f"], g[name + "zi"], g[name + "z"], g[name + "x"],
-        g[name + "ss"], g[name + "rs"],
-    )
-    red.zin_out = g[name + "zo"]
-    return red
+    d, f, x, z, y, c = place(zn)
+    _, zs, _ = ring_peers(xn, zn, yn)
+    group, me = plane_group(xn, zn, yn)
+    others = [(g[name + "z"], zs, z)]
+    return Exchange(group, me, g[name + "src"], out, g[name + "f"], others, g[name + "ss"], g[name + "rs"])
 
 
 def put_slices(ref, index, value):
@@ -266,8 +248,8 @@
     up_y, down_y = (d, yu * CORES + c), (d, yd * CORES + c)
     above, below = ((d + 1) % dn, f), ((d + dn - 1) % dn, f)
     tiles, size = m.adjv.shape[0], m.adjv.shape[1]
-    w = m.x.shape[1]
-    blocks = m.x.shape[0] // size
+    w = m.xv.shape[1]
+    blocks = m.xv.shape[0] // size
     nown = blocks * yn * CORES
     nb = m.lists.shape[1]
     next_ = nown + 2 * nb
@@ -282,45 +264,18 @@
         singles.append(copy)
         return copy
 
-    peers = feat + zs + xs + [above, below]
     barrier = pltpu.get_barrier_semaphore()
+    plane, _ = plane_group(xn, zn, yn)
+    peers = [peer for _, peer in plane] + zs + [above, below]
     for peer in peers:
         pl.semaphore_signal(barrier, inc=1, device_id=peer, device_id_type=MESH)
-    fetch = pltpu.make_async_copy(m.adj, m.adjv, m.ls.at[0])
-    fetch.start()
-
-    xv = m.x[...]
-    key_proj = dot(xv, m.wk[...])
-    kf = feature(key_proj).astype(BF16)
-    vf = dot(xv, m.wv[...]).astype(BF16)
-    m.kf[...] = kf
-    m.vf[...] = vf
-    state_store(m.asrc, compact(dot_tn(kf, vf)), jnp.sum(kf.astype(F32), axis=0, keepdims=True))
-    xblocks = xv.reshape(blocks, size, w)
-    m.xo[pl.ds(f * blocks, blocks)] = xblocks
-
-    pl.semaphore_wait(barrier, len(peers))
-
-    red1 = state_sum("a", xn, zn, yn, m, m.ast)
-    red2 = state_sum("b", xn, zn, yn, m, m.st2)
-    sum1 = grad_sum("c", xn, zn, yn, m, m.g1)
-    sum2 = grad_sum("e", xn, zn, yn, m, m.g2)
-    red1.scatter()
-
-    def chunk(yy, h, count=1):
-        return m.xo.at[pl.ds((yy * CORES + c) * blocks + h * hb, hb * count)]
-
-    a0 = go(0, chunk(y, 0), chunk(y, 0), up_y)
-    b1 = go(1, chunk(y, 1), chunk(y, 1), down_y)
-    a1 = go(2, chunk(y, 1), chunk(y, 1), up_y)
-    b0 = go(3, chunk(y, 0), chunk(y, 0), down_y)
-    s_own = go(4, chunk(y, 0, 2), chunk(y, 0, 2), sibling)
-
-    m.qf[...] = feature(dot(xv, m.wq[...])).astype(BF16)
-    zero = jnp.zeros((size, w), BF16)
-    for b in range(blocks):
-        m.g5[b] = (m.cot[b * size : (b + 1) * size, :].astype(F32) * 0.5).astype(BF16)
-    m.g5[blocks] = zero
+    inputs = (
+        (m.x, m.xv), (m.wk, m.wkv), (m.wv, m.wvv), (m.cot, m.cotv), (m.adj, m.adjv), (m.wq, m.wqv), (m.wg, m.wgv),
+    )
+    fetch = [pltpu.make_async_copy(a, b, m.ls.at[i]) for i, (a, b) in enumerate(inputs)]
+    for copy in fetch:
+        copy.start()
+
     tpad = -(-tiles // 8) * 8
     down = lax.broadcasted_iota(jnp.int32, (tpad, 128), 0)
     across = lax.broadcasted_iota(jnp.int32, (tpad, 128), 1)
@@ -338,27 +293,51 @@
 
     order = chains(m.cols) + chains(m.rows)
     m.ordv[...] = jnp.concatenate(order + order, 0)
-    index = pltpu.make_async_copy(m.ordv, m.ords, m.ls.at[1])
+    index = pltpu.make_async_copy(m.ordv, m.ords, m.ls.at[7])
     index.start()
+
+    for copy in fetch[:3]:
+        copy.wait()
+    xv = m.xv[...]
+    kf = feature(dot(xv, m.wkv[...])).astype(BF16)
+    vf = dot(xv, m.wvv[...]).astype(BF16)
+    m.kf[...] = kf
+    m.vf[...] = vf
+    state_store(m.asrc, compact(dot_tn(kf, vf)), jnp.sum(kf.astype(F32), axis=0, keepdims=True))
+    m.xo[pl.ds(f * blocks, blocks)] = xv.reshape(blocks, size, w)
+    for copy in fetch[3:]:
+        copy.wait()
     index.wait()
-    fetch.wait()
-
+    for b in range(blocks):
+        m.g5[b] = (m.cotv[b * size : (b + 1) * size, :].astype(F32) * 0.5).astype(BF16)
+    m.g5[blocks] = jnp.zeros((size, w), BF16)
     m.prod[tiles] = jnp.zeros((size, w), F32)
-    step = tiles // 4
+
+    red1 = state_sum("a", xn, zn, yn, m, m.ast)
+    red2 = state_sum("b", xn, zn, yn, m, m.bst)
+    sum1 = grad_sum("c", xn, zn, yn, m, m.cout)
+    sum2 = grad_sum("e", xn, zn, yn, m, m.eout)
+
+    pl.semaphore_wait(barrier, len(peers))
+    red1.scatter()
+
+    def chunk(yy, h, count=1):
+        return m.xo.at[pl.ds((yy * CORES + c) * blocks + h * hb, hb * count)]
+
+    a0 = go(0, chunk(y, 0), chunk(y, 0), up_y)
+    b1 = go(1, chunk(y, 1), chunk(y, 1), down_y)
+    a1 = go(2, chunk(y, 1), chunk(y, 1), up_y)
+    b0 = go(3, chunk(y, 0), chunk(y, 0), down_y)
+    s_own = go(4, chunk(y, 0, 2), chunk(y, 0, 2), sibling)
+
+    step = tiles // 2
 
     def back_one(t, carry):
         m.prod[t] = dot_tn(m.adjv[t], m.g5[m.rows[t]]) + m.prod[m.ords[0, t]]
         return carry
 
     def back_tiles(part):
-        lax.fori_loop(part * step, (part + 1) * step, back_one, 0, unroll=4)
-
-    back_tiles(0)
-    back_tiles(1)
-    red1.along_z()
-    back_tiles(2)
-    back_tiles(3)
-    red1.along_x()
+        lax.fori_loop(part * step, (part + 1) * step, back_one, 0, unroll=step)
 
     def to_sibling(start, count):
         def one(i, carry):
@@ -367,17 +346,19 @@
 
         lax.fori_loop(0, count, one, 0)
 
+    back_tiles(0)
+    back_tiles(1)
+    red1.along(0)
+    to_sibling(nown, 2 * nb)
+    sib_rim = go(7, m.pext.at[pl.ds(nown, 2 * nb)], m.sib.at[pl.ds(nown, 2 * nb)], sibling)
     a0.wait_recv()
     fa = go(5, chunk(yd, 0), chunk(yd, 0), up_y)
+    s0 = go(8, chunk(yd, 0), chunk(yd, 0), sibling)
     b1.wait_recv()
     fb = go(6, chunk(yu, 1), chunk(yu, 1), down_y)
-    to_sibling(nown, 2 * nb)
-    sib_rim = go(7, m.pext.at[pl.ds(nown, 2 * nb)], m.sib.at[pl.ds(nown, 2 * nb)], sibling)
-    s0 = go(8, chunk(yd, 0), chunk(yd, 0), sibling)
     s1 = go(9, chunk(yu, 1), chunk(yu, 1), sibling)
     to_sibling(0, nown)
     sib_own = go(10, m.pext.at[pl.ds(0, nown)], m.sib.at[pl.ds(0, nown)], sibling)
-    red1.gather()
 
     sib_rim.wait_recv()
 
@@ -390,10 +371,27 @@
     to_below = go(11, m.rimsum.at[pl.ds(0, nb)], m.back.at[0], below)
     to_above = go(12, m.rimsum.at[pl.ds(nb, nb)], m.back.at[1], above)
 
+    red1.along(1)
+    xv = m.xv[...]
+    m.qf[...] = feature(dot(xv, m.wqv[...])).astype(BF16)
     a1.wait_recv()
     s2 = go(13, chunk(yd, 1), chunk(yd, 1), sibling)
     b0.wait_recv()
     s3 = go(14, chunk(yu, 0), chunk(yu, 0), sibling)
+    put_slices(m.csrc, 1, dot_tn(xv, m.kf[...]))
+    red1.gather()
+
+    fa.wait_recv()
+    s4 = go(15, chunk(yo, 0), chunk(yo, 0), sibling)
+    fb.wait_recv()
+    s5 = go(16, chunk(yo, 1), chunk(yo, 1), sibling)
+    for copy in (s_own, s0, s1, s2, s3, s4, s5):
+        copy.wait_recv()
+    for s in range(nb):
+        m.picks[0, s] = m.xo[m.lists[1, s], keep]
+        m.picks[1, s] = m.xo[m.lists[0, s], keep]
+    f_above = go(17, m.picks.at[0], m.xr.at[0, :, keep], above)
+    f_below = go(18, m.picks.at[1], m.xr.at[1, :, keep], below)
 
     red1.arrive()
     small, ks = state_load(m.ast)
@@ -404,7 +402,7 @@
     q = m.qf[...]
     rden = 1.0 / dots(dot, [q], ks_bd)
     attn = dots(dot, [q], kv) * rden
-    g = m.cot[...].astype(F32) * 0.5
+    g = m.cotv[...].astype(F32) * 0.5
     ones = jnp.where(head, 1.0, 0.0).astype(BF16)
     dden = -dots(dot, split(g * attn, 3), [ones]) * rden
     dstate = compact(dots(dot_tn, [q], split(g * rden, 3)))
@@ -412,27 +410,10 @@
     red2.scatter()
     m.attn[...] = attn
     dqf = dots(dot_nt, [g.astype(BF16)], kv) * rden + dden * ks
-    dq = dqf * slope(dot(m.x[...], m.wq[...]))
+    xv = m.xv[...]
+    dq = dqf * slope(dot(xv, m.wqv[...]))
     m.dq[...] = dq
-
-    fa.wait_recv()
-    s4 = go(15, chunk(yo, 0), chunk(yo, 0), sibling)
-    fb.wait_recv()
-    s5 = go(16, chunk(yo, 1), chunk(yo, 1), sibling)
-
-    xv = m.x[...]
     put_slices(m.csrc, 0, dots(dot_tn, [xv], split(dq, 2)))
-    put_slices(m.csrc, 1, dot_tn(xv, m.kf[...]))
-    red2.along_z()
-
-    for copy in (s_own, s0, s1, s2, s3, s4, s5):
-        copy.wait_recv()
-    for s in range(nb):
-        m.picks[0, s] = m.xo[m.lists[1, s], keep]
-        m.picks[1, s] = m.xo[m.lists[0, s], keep]
-    f_above = go(17, m.picks.at[0], m.xr.at[0, :, keep], above)
-    f_below = go(18, m.picks.at[1], m.xr.at[1, :, keep], below)
-    sum1.scatter()
 
     sib_own.wait_recv()
     to_below.wait_recv()
@@ -467,15 +448,24 @@
     y0 = go(19, piece(yo, 0), m.ybuf.at[0], up_y)
     place_rims(yo * per + blocks)
     y1 = go(20, piece(yo, 1), m.ybuf.at[1], down_y)
-    red2.along_x()
+    red2.along(0)
     place_rims(yu * per + blocks)
     y2 = go(21, piece(yu, 1), m.ybuf.at[2], up_y)
     place_rims(yd * per)
     y3 = go(22, piece(yd, 0), m.ybuf.at[3], down_y)
     place_rims(yu * per)
     place_rims(yd * per + blocks)
-    red2.gather()
-    sum1.along_z()
+
+    def project(value, start):
+        count = value.shape[0]
+        here = pl.ds(start, count)
+        m.xp[here] = value
+        value = dot(value.reshape(count * size, w), m.wgv[...])
+        m.ext[here] = value.astype(BF16).reshape(count, size, w)
+
+    project(m.xo[: nown // 2], 0)
+    red2.along(1)
+    sum1.scatter()
 
     def add_piece(n, base):
         def one(i, carry):
@@ -484,6 +474,20 @@
 
         lax.fori_loop(0, blocks, one, 0)
 
+    red2.gather()
+    f_above.wait_recv()
+    f_below.wait_recv()
+
+    @pl.when(d == 0)
+    def _():
+        m.xr[0, :, keep] = jnp.zeros((nb, half, w), BF16)
+
+    @pl.when(d == dn - 1)
+    def _():
+        m.xr[1, :, keep] = jnp.zeros((nb, half, w), BF16)
+
+    s6 = go(25, m.xr.at[0, :, keep], m.xr.at[0, :, keep], sibling)
+    s7 = go(26, m.xr.at[1, :, keep], m.xr.at[1, :, keep], sibling)
     y0.wait_recv()
     add_piece(0, yu * per)
     y4 = go(23, m.ysum.at[0], m.ybuf.at[4], up_y)
@@ -492,46 +496,11 @@
     y5 = go(24, m.ysum.at[1], m.ybuf.at[5], down_y)
     place_rims(y * per)
     place_rims(y * per + blocks)
-
-    def project(value, start):
-        here = pl.ds(start, blocks)
-        m.xp[here] = value
-        value = dot(value.reshape(blocks * size, w), m.wg[...])
-        m.ext[here] = value.astype(BF16).reshape(blocks, size, w)
-
-    def project_own(i, carry):
-        project(m.xo[pl.ds(i * blocks, blocks)], i * blocks)
-        return carry
-
-    lax.fori_loop(0, nown // blocks, project_own, 0)
-    f_above.wait_recv()
-    f_below.wait_recv()
-
-    @pl.when(d == 0)
-    def _():
-        m.xr[0, :, keep] = jnp.zeros((nb, half, w), BF16)
-
-    @pl.when(d == dn - 1)
-    def _():
-        m.xr[1, :, keep] = jnp.zeros((nb, half, w), BF16)
-
-    s6 = go(25, m.xr.at[0, :, keep], m.xr.at[0, :, keep], sibling)
-    s7 = go(26, m.xr.at[1, :, keep], m.xr.at[1, :, keep], sibling)
-    sum1.along_x()
-
-    red2.arrive()
-    small, dks = state_load(m.st2)
-    ds = split(block_diag(small), 2)
-    xv = m.x[...]
-    dk = (dots(dot_nt, [m.vf[...]], ds) + dks) * slope(dot(xv, m.wk[...]))
-    put_slices(m.esrc, 0, dots(dot_tn, [xv], split(dk, 2)))
-    m.dk[...] = dk
-
+    project(m.xo[nown // 2 :], nown // 2)
     s6.wait_recv()
     s7.wait_recv()
     for side in range(2):
-        for i in range(nb // blocks):
-            project(m.xr[side, i * blocks : (i + 1) * blocks], nown + side * nb + i * blocks)
+        project(m.xr[side], nown + side * nb)
     m.fprod[tiles] = jnp.zeros((size, w), F32)
     m.xprod[tiles] = jnp.zeros((size, w), F32)
 
@@ -543,20 +512,38 @@
         m.xprod[t] = dot(tile, m.xp[b]) + m.xprod[before]
         return carry
 
-    lax.fori_loop(0, tiles // 2, fore_one, 0, unroll=4)
-    sum1.back_z()
-    lax.fori_loop(tiles // 2, tiles, fore_one, 0, unroll=4)
+    lax.fori_loop(0, tiles, fore_one, 0, unroll=tiles // 2)
     graph = None
     for b in range(blocks):
-        here = slice(b * size, (b + 1) * size)
         term = dots(dot_tn, split(m.xprod[m.ords[3, b]], 2), [m.g5[b]])
         graph = term if graph is None else graph + term
     put_slices(m.esrc, 1, graph)
+
+    red2.arrive()
+    small, dks = state_load(m.bst)
+    ds = split(block_diag(small), 2)
+    xv = m.xv[...]
+    dk = (dots(dot_nt, [m.vf[...]], ds) + dks) * slope(dot(xv, m.wkv[...]))
+    put_slices(m.esrc, 0, dots(dot_tn, [xv], split(dk, 2)))
     sum2.scatter()
-    sum1.gather()
+    sum1.along(0)
+
     for b in range(blocks):
         here = slice(b * size, (b + 1) * size)
-        m.layer[here, :] = (0.5 * m.attn[here, :] + 0.5 * m.fprod[m.ords[3, b]]).astype(BF16)
+        m.layerv[here, :] = (0.5 * m.attn[here, :] + 0.5 * m.fprod[m.ords[3, b]]).astype(BF16)
+    outs = [
+        pltpu.make_async_copy(m.layerv, m.layer, m.ls.at[8]),
+        pltpu.make_async_copy(m.bst, m.st2, m.ls.at[9]),
+    ]
+    for copy in outs:
+        copy.start()
+    dv = dots(dot, [m.kf[...]], ds)
+    total = None
+    for grad, weight in ((m.dq[...], m.wqv), (dk, m.wkv), (dv, m.wvv)):
+        term = dots(dot_nt, split(grad, 2), [weight[...]])
+        total = term if total is None else total + term
+
+    sum2.along(0)
 
     for copy in (y2, y3, y4, y5):
         copy.wait_recv()
@@ -572,24 +559,25 @@
     lax.fori_loop(0, blocks, last, 0)
     pg_copy = go(27, m.res.at[pl.ds(blocks * (1 - c), blocks)], m.pg.at[:, keep], sibling)
     m.pg[:, keep] = m.res[pl.ds(blocks * c, blocks)]
-    sum2.along_z()
-    dv = dots(dot, [m.kf[...]], ds)
-    total = None
-    for grad, weight in ((m.dq[...], m.wq), (m.dk[...], m.wk), (dv, m.wv)):
-        term = dots(dot_nt, split(grad, 2), [weight[...]])
-        total = term if total is None else total + term
-    sum2.along_x()
+    sum1.gather()
     pg_copy.wait_recv()
-    total = total + dots(dot_nt, split(m.pg[...].reshape(blocks * size, w), 2), [m.wg[...]])
-    m.gfeat[...] = total.astype(BF16)
-    sum2.back_z()
+    total = total + dots(dot_nt, split(m.pg[...].reshape(blocks * size, w), 2), [m.wgv[...]])
+    m.gfeatv[...] = total.astype(BF16)
+    outs.append(pltpu.make_async_copy(m.gfeatv, m.gfeat, m.ls.at[10]))
+    outs[2].start()
     sum2.gather()
     sum1.arrive()
+    outs.append(pltpu.make_async_copy(m.cout, m.g1, m.ls.at[11]))
+    outs[3].start()
     sum2.arrive()
+    outs.append(pltpu.make_async_copy(m.eout, m.g2, m.ls.at[12]))
+    outs[4].start()
     for red in (red1, red2, sum1, sum2):
         red.finish()
     for copy in singles:
         copy.wait_send()
+    for copy in outs:
+        copy.wait()
 
 
 def last_kernel(layer_i, gfeat_i, c1, c2, st, layer, gfeat, gq, gk, gv, gg):
@@ -606,8 +594,7 @@
     gk[...] = mat(c2, 0)
     gg[...] = mat(c2, 1)
     small, _ = state_load(st)
-    ds = split(block_diag(small), 2)
-    gv[...] = dots(dot, split(mat(c1, 1), 2), ds)
+    gv[...] = dots(dot, split(mat(c1, 1), 2), split(block_diag(small), 2))
 
 
 def shards(xn, zn, x, wq, wk, wv, wg, adj, rows, cols, lists, cot):
@@ -622,22 +609,34 @@
     S = jax.ShapeDtypeStruct
     V = pltpu.VMEM
     half = size // 2
-    part = 2 * w // (yn * CORES)
+    owners = yn * CORES * xn
+    part = 2 * w // owners
     singles = 28
 
     ins = [
-        ("rows", SM), ("cols", SM), ("lists", SM), ("x", VM), ("wq", VM), ("wk", VM), ("wv", VM), ("wg", VM),
-        ("cot", VM), ("adj", HB),
+        ("rows", SM), ("cols", SM), ("lists", SM), ("x", HB), ("wq", HB), ("wk", HB), ("wv", HB), ("wg", HB),
+        ("cot", HB), ("adj", HB),
     ]
     outs = [
         ("layer", S((n, w), BF16)),
         ("gfeat", S((n, w), BF16)),
-        ("g1", S((yn * CORES, part, w), BF16)),
-        ("g2", S((yn * CORES, part, w), BF16)),
+        ("g1", S((owners, part, w), BF16)),
+        ("g2", S((owners, part, w), BF16)),
         ("st2", S((8, 8, w), F32)),
     ]
     scratch = [
+        ("xv", V((n, w), BF16)),
+        ("wqv", V((w, w), BF16)),
+        ("wkv", V((w, w), BF16)),
+        ("wvv", V((w, w), BF16)),
+        ("wgv", V((w, w), BF16)),
+        ("cotv", V((n, w), BF16)),
         ("adjv", V((tiles, size, size), BF16)),
+        ("layerv", V((n, w), BF16)),
+        ("gfeatv", V((n, w), BF16)),
+        ("cout", V((owners, part, w), BF16)),
+        ("eout", V((owners, part, w), BF16)),
+        ("bst", V((8, 8, w), F32)),
         ("kf", V((n, w), BF16)),
         ("vf", V((n, w), BF16)),
         ("qf", V((n, w), BF16)),
@@ -661,11 +660,10 @@
         ("pg", V((blocks, size, w), F32)),
         ("attn", V((n, w), F32)),
         ("dq", V((n, w), F32)),
-        ("dk", V((n, w), F32)),
         ("ast", V((8, 8, w), F32)),
         ("ordv", V((8, 128), jnp.int32)),
         ("ords", pltpu.SMEM((8, 128), jnp.int32)),
-        ("ls", pltpu.SemaphoreType.DMA((2,))),
+        ("ls", pltpu.SemaphoreType.DMA((13,))),
         ("ss", pltpu.SemaphoreType.DMA((singles,))),
         ("rs", pltpu.SemaphoreType.DMA((singles,))),
     ]
@@ -676,7 +674,7 @@
         functools.partial(layer_kernel, names, xn, zn, yn),
         out_shape=[shape for _, shape in outs],
         in_specs=[spec for _, spec in ins],
-        out_specs=[VM] * len(outs),
+        out_specs=[HB] * len(outs),
         scratch_shapes=[shape for _, shape in scratch],
         compiler_params=pltpu.CompilerParams(
             collective_id=0, has_side_effects=True, vmem_limit_bytes=LIMIT

time: 84.4 us -> 77.4 us (0.917)
  Pallas kernels: 83.6 us -> 76.6 us
    pallas_call x1, Pallas kernels: 81.1 us -> 74 us  [shards(): pl.pallas_call(functools.partial(layer_kernel, names, xn, zn, yn), out_sh...]
where the time goes in v3:
time: 77.4 us; the launch traced here: 77.2 us
  Pallas kernels  76.6 us (99%)
    pallas_call x1, Pallas kernels, shards(): pl.pallas_call(functools.partial(layer_kernel, names, xn, zn, yn), out_sh...  74 us
    pallas_call x1, Pallas kernels, shards(): pl.pallas_call(last_kernel, out_shape=[S((n, w), BF16)] * 2 + [S((w, w),...  2.58 us

profile of v3, /device:TPU:1, one launch (start us, length us, event | category | flops | bytes accessed | tf_op | source)
XLA Modules:
  0.0 77.2 jit_solution(8199495234463830148)
XLA Ops:
  0.6 74.0 %layer.1 = (bf16[512,256]{1,0:T(8,128)(2,1)}, bf16[512,256]{1,0:T(8,128)(2,1)}, bf16[32,16,256]{2,1,0:T(8,128)(2,1)}, bf16[32,16,256]{2,1,0:T(8,128)(2,1)}, f32[8,8,256]{2,1,0:T(8,128)}) custom-call(s32[48]{0:T(128)} %refs_0_.1, s32[48]{0:T(128)} %refs_1_.1, s32[2,8]{1,0:T(2,128)} %bitcast.1, bf16[512,256]{1,0:T(8,128)(2,1)} %refs_3_.1, ...), custom_call_target="tpu_custom_call" | custom-call | tf_op jit(solution)/shard_map/layer/pallas_call | solution.py:673
  74.6 2.6 %last.1 = (bf16[512,256]{1,0:T(8,128)(2,1)}, bf16[512,256]{1,0:T(8,128)(2,1)}, f32[256,256]{1,0:T(8,128)}, f32[256,256]{1,0:T(8,128)}, f32[256,256]{1,0:T(8,128)}, /*index=5*/f32[256,256]{1,0:T(8,128)}) custom-call(bf16[512,256]{1,0:T(8,128)(2,1)} %get-tuple-element.11.layer_i, bf16[512,256]{1,0:T(8,128)(2,1)} %get-tuple-element.12.gfeat_i, ...), custom_call_target="tpu_custom_call" | custom-call | tf_op jit(solution)/shard_map/last/pallas_call | solution.py:685

commit v4 on v3

--- a/solution.py
+++ b/solution.py
@@ -125,8 +125,9 @@
 
 
 class Exchange:
-    def __init__(self, group, me, src, out, fbuf, others, ssem, rsem):
+    def __init__(self, group, me, src, out, fbuf, others, ssem, rsem, gather=None):
         self.group, self.me = group, me
+        self.gather_group, self.gather_me = gather or (group, me)
         self.src, self.out, self.fbuf, self.others = src, out, fbuf, others
         self.ssem, self.rsem = ssem, rsem
         self.used = 0
@@ -166,9 +167,10 @@
         self.spread([buf.at[me]] * len(peers), buf.at[me], peers)
 
     def gather(self):
-        self.out[self.me] = self.total().astype(self.out.dtype)
-        here = self.out.at[self.me]
-        self.spread([here] * len(self.group), here, [p for _, p in self.group])
+        me, group = self.gather_me, self.gather_group
+        self.out[me] = self.total().astype(self.out.dtype)
+        here = self.out.at[me]
+        self.spread([here] * len(group), here, [p for _, p in group])
 
     def finish(self):
         for copy in self.sent:
@@ -187,48 +189,92 @@
     return group, x * n + f
 
 
-def state_scratch(name, xn, zn, yn, w):
-    count = 2 * (yn * CORES - 1) + zn - 1 + xn - 1
-    return [
-        (name + "src", pltpu.VMEM((8, 8, w), F32)),
-        (name + "f", pltpu.VMEM((8, 8, w), F32)),
-        (name + "z", pltpu.VMEM((zn, 8, w), F32)),
-        (name + "x", pltpu.VMEM((xn, 8, w), F32)),
+def sum_scratch(name, first, xn, zn, shape, kind, count, third=False):
+    out = [
+        (name + "src", pltpu.VMEM((first, *shape), kind)),
+        (name + "z", pltpu.VMEM((zn, *shape), F32)),
         (name + "ss", pltpu.SemaphoreType.DMA((count,))),
         (name + "rs", pltpu.SemaphoreType.DMA((count,))),
     ]
-
-
-def grad_scratch(name, xn, zn, yn, rows, w):
-    n = yn * CORES * xn
-    count = 2 * (n - 1) + zn - 1
-    part = rows // n
-    return [
-        (name + "src", pltpu.VMEM((n, part, w), BF16)),
-        (name + "f", pltpu.VMEM((n, part, w), BF16)),
-        (name + "z", pltpu.VMEM((zn, part, w), F32)),
-        (name + "ss", pltpu.SemaphoreType.DMA((count,))),
-        (name + "rs", pltpu.SemaphoreType.DMA((count,))),
-    ]
-
-
-def state_sum(name, xn, zn, yn, m, out):
-    g = vars(m)
+    if first > 1 or not third:
+        out.append((name + "f", pltpu.VMEM((first, *shape), kind)))
+    if third:
+        out.append((name + "x", pltpu.VMEM((xn, *shape), F32)))
+    return out
+
+
+def make_sums(xn, zn, yn, m):
     d, f, x, z, y, c = place(zn)
     feat, zs, xs = ring_peers(xn, zn, yn)
-    n = len(feat) + 1
-    group = [((f + k) % n, feat[k - 1]) for k in range(1, n)]
-    others = [(g[name + "z"], zs, z), (g[name + "x"], xs, x)]
-    return Exchange(group, f, g[name + "src"], out, g[name + "f"], others, g[name + "ss"], g[name + "rs"])
-
-
-def grad_sum(name, xn, zn, yn, m, out):
-    g = vars(m)
-    d, f, x, z, y, c = place(zn)
-    _, zs, _ = ring_peers(xn, zn, yn)
-    group, me = plane_group(xn, zn, yn)
-    others = [(g[name + "z"], zs, z)]
-    return Exchange(group, me, g[name + "src"], out, g[name + "f"], others, g[name + "ss"], g[name + "rs"])
+    n = yn * CORES
+    fgroup = [((f + k) % n, feat[k - 1]) for k in range(1, n)]
+    xgroup = [((x + k) % xn, xs[k - 1]) for k in range(1, xn)]
+    plane, pme = plane_group(xn, zn, yn)
+    red1 = Exchange(fgroup, f, m.asrc, m.ast, m.af, [(m.az, zs, z), (m.ax, xs, x)], m.ass, m.ars)
+    red2 = Exchange(fgroup, f, None, m.bst, m.bsrc, [(m.bz, zs, z), (m.bx, xs, x)], m.bss, m.brs)
+    cots = Exchange(fgroup, f, m.gsrc, None, m.gf, [], m.gss, m.grs)
+    sum1 = Exchange(plane, pme, m.csrc, m.cout, m.cf, [(m.cz, zs, z)], m.css, m.crs)
+    sum2 = Exchange(plane, pme, m.esrc, m.eout, m.ef, [(m.ez, zs, z)], m.ess, m.ers)
+    keys = Exchange(xgroup, x, m.ksrc, m.kout, m.kf_, [(m.kz, zs, z)], m.kss, m.krs, (plane, pme))
+    return red1, red2, cots, sum1, sum2, keys
+
+
+def lanes(rows, cols):
+    return (
+        lax.broadcasted_iota(jnp.int32, (rows, cols), 0),
+        lax.broadcasted_iota(jnp.int32, (rows, cols), 1),
+    )
+
+
+def ones_where(mask):
+    return jnp.where(mask, 1.0, 0.0).astype(BF16)
+
+
+def fold_ones():
+    r, c = lanes(128, 128)
+    return ones_where(r % HD == c % HD)
+
+
+def fold_rows(value, groups):
+    n = value.shape[0] // groups
+    lane = lanes(n, 128)[1] // HD
+    out = jnp.zeros((n, 128), F32)
+    for q in range(groups):
+        out = out + jnp.where(lane == q, value[q * n : (q + 1) * n], 0.0)
+    return out
+
+
+def open_rows(value):
+    lane = lanes(value.shape[0], 128)[1] // HD
+    return jnp.concatenate([jnp.where(lane == q, value, jnp.zeros((), value.dtype)) for q in range(4)], 0)
+
+
+def square(rows):
+    return jnp.where(same_head(128, 128), jnp.concatenate([rows] * 4, 0), 0.0)
+
+
+def open_states(ref):
+    rows = jnp.concatenate([open_rows(ref[h][0:8]) for h in range(HEADS)], 0)
+    rows = dots(dot, split(rows, 3), [fold_ones()])
+    width = HEADS * HD
+    state = jnp.where(same_head(width, width), jnp.concatenate([rows] * (width // 128), 1), 0.0)
+    lane = lanes(1, width)[1] // HD
+    ks = jnp.zeros((1, width), F32)
+    for h in range(HEADS):
+        ks = ks + jnp.where(lane == h, jnp.concatenate([ref[h][8:9]] * (width // 128), 1), 0.0)
+    return state, ks
+
+
+def attention(q, g, state, ks):
+    width = ks.shape[1]
+    kv = split(state, 3)
+    head = same_head(width, width)
+    ks_col = jnp.broadcast_to(ks, (128, width)).T
+    ks_bd = split(jnp.where(head, jnp.concatenate([ks_col] * (width // 128), 1), 0.0), 3)
+    rden = 1.0 / dots(dot, [q], ks_bd)
+    attn = dots(dot, [q], kv) * rden
+    dden = -dots(dot, split(g * attn, 3), [ones_where(head)]) * rden
+    return attn, rden, dden, kv
 
 
 def put_slices(ref, index, value):
@@ -303,20 +349,31 @@
     vf = dot(xv, m.wvv[...]).astype(BF16)
     m.kf[...] = kf
     m.vf[...] = vf
-    state_store(m.asrc, compact(dot_tn(kf, vf)), jnp.sum(kf.astype(F32), axis=0, keepdims=True))
+    ksum = jnp.sum(kf.astype(F32), axis=0, keepdims=True)
+    local = jnp.concatenate([compact(dot_tn(kf, vf)), jnp.broadcast_to(ksum, (8, w))], 0)
+    er, ec = lanes(w, HEADS * 128)
+    pick = (ec // 128 == er // HD) & (ec % HD == er % HD)
+    local = dots(dot, split(local, 3), [ones_where(pick)])
+    for h in range(HEADS):
+        here = local[:, h * 128 : (h + 1) * 128]
+        m.asrc[h] = jnp.concatenate([fold_rows(here[:HD], 4), here[HD : HD + 1]], 0)
     m.xo[pl.ds(f * blocks, blocks)] = xv.reshape(blocks, size, w)
     for copy in fetch[3:]:
         copy.wait()
+    packed = None
+    for b in range(blocks):
+        chosen = ones_where(pick & (ec % 128 // HD == b))
+        term = dot(m.cotv[b * size : (b + 1) * size, :], chosen)
+        packed = term if packed is None else packed + term
+    for h in range(HEADS):
+        m.gsrc[h] = packed[:, h * 128 : (h + 1) * 128].astype(BF16)
     index.wait()
     for b in range(blocks):
         m.g5[b] = (m.cotv[b * size : (b + 1) * size, :].astype(F32) * 0.5).astype(BF16)
     m.g5[blocks] = jnp.zeros((size, w), BF16)
     m.prod[tiles] = jnp.zeros((size, w), F32)
 
-    red1 = state_sum("a", xn, zn, yn, m, m.ast)
-    red2 = state_sum("b", xn, zn, yn, m, m.bst)
-    sum1 = grad_sum("c", xn, zn, yn, m, m.cout)
-    sum2 = grad_sum("e", xn, zn, yn, m, m.eout)
+    red1, red2, cots, sum1, sum2, keys = make_sums(xn, zn, yn, m)
 
     pl.semaphore_wait(barrier, len(peers))
     red1.scatter()
@@ -329,6 +386,7 @@
     a1 = go(2, chunk(y, 1), chunk(y, 1), up_y)
     b0 = go(3, chunk(y, 0), chunk(y, 0), down_y)
     s_own = go(4, chunk(y, 0, 2), chunk(y, 0, 2), sibling)
+    cots.scatter()
 
     step = tiles // 2
 
@@ -393,27 +451,41 @@
     f_above = go(17, m.picks.at[0], m.xr.at[0, :, keep], above)
     f_below = go(18, m.picks.at[1], m.xr.at[1, :, keep], below)
 
-    red1.arrive()
-    small, ks = state_load(m.ast)
-    kv = split(block_diag(small), 3)
-    ks_col = jnp.broadcast_to(ks, (128, w)).T
-    head = same_head(w, w)
-    ks_bd = split(jnp.where(head, jnp.concatenate([ks_col] * (w // 128), 1), 0.0), 3)
-    q = m.qf[...]
-    rden = 1.0 / dots(dot, [q], ks_bd)
-    attn = dots(dot, [q], kv) * rden
-    g = m.cotv[...].astype(F32) * 0.5
-    ones = jnp.where(head, 1.0, 0.0).astype(BF16)
-    dden = -dots(dot, split(g * attn, 3), [ones]) * rden
-    dstate = compact(dots(dot_tn, [q], split(g * rden, 3)))
-    state_store(m.bsrc, dstate, jnp.sum(dden * q.astype(F32), axis=0, keepdims=True))
-    red2.scatter()
-    m.attn[...] = attn
-    dqf = dots(dot_nt, [g.astype(BF16)], kv) * rden + dden * ks
-    xv = m.xv[...]
-    dq = dqf * slope(dot(xv, m.wqv[...]))
-    m.dq[...] = dq
-    put_slices(m.csrc, 0, dots(dot_tn, [xv], split(dq, 2)))
+    count = yn * CORES
+    fold = fold_ones()
+    hr, hc = lanes(w, 128)
+    chosen = [ones_where((hr == f * HD + hc % HD) & (hc // HD == b)) for b in range(blocks)]
+
+    def part_rows(b):
+        return jnp.concatenate([m.xo[p * blocks + b] for p in range(count)], 0)
+
+    def by_head(weights):
+        total = None
+        for b in range(blocks):
+            weight = jnp.concatenate([dot(v[...], chosen[b]).astype(BF16) for v in weights], 1)
+            term = dot(part_rows(b), weight)
+            total = term if total is None else total + term
+        return total
+
+    hq = feature(by_head([m.wqv])).astype(BF16)
+    cots.arrive()
+    hg = m.gf[...].reshape(count * size, 128).astype(F32) * 0.5
+    mine = m.ast[f]
+    hstate = square(dots(dot, split(open_rows(mine[0:8]), 3), [fold]))
+    _, rden, dden, _ = attention(hq, hg, hstate, mine[8:9])
+    full = dots(dot_tn, [hq], split(hg * rden, 3))
+    group = lanes(HD, 128)[1] // HD
+    small = jnp.zeros((HD, 128), F32)
+    for b in range(blocks):
+        small = small + jnp.where(group == b, full[b * HD : (b + 1) * HD], 0.0)
+    dsum = jnp.sum(dden * hq.astype(F32), axis=0, keepdims=True)
+    both = jnp.concatenate([small, jnp.broadcast_to(dsum, (8, 128))], 0)
+    both = dots(dot, split(both, 3), [fold])
+    m.bsrc[0] = jnp.concatenate([fold_rows(both[:HD], 4), both[HD : HD + 1]], 0)
+    red2.along(0)
+    hkv = by_head([m.wkv, m.wvv])
+    m.hkey[...] = hkv[:, :128]
+    m.hval[...] = hkv[:, 128:].astype(BF16)
 
     sib_own.wait_recv()
     to_below.wait_recv()
@@ -448,7 +520,6 @@
     y0 = go(19, piece(yo, 0), m.ybuf.at[0], up_y)
     place_rims(yo * per + blocks)
     y1 = go(20, piece(yo, 1), m.ybuf.at[1], down_y)
-    red2.along(0)
     place_rims(yu * per + blocks)
     y2 = go(21, piece(yu, 1), m.ybuf.at[2], up_y)
     place_rims(yd * per)
@@ -463,10 +534,19 @@
         value = dot(value.reshape(count * size, w), m.wgv[...])
         m.ext[here] = value.astype(BF16).reshape(count, size, w)
 
-    project(m.xo[: nown // 2], 0)
+    red1.arrive()
+    state, ks = open_states(m.ast)
+    g = m.cotv[...].astype(F32) * 0.5
+    attn, rden, dden, kv = attention(m.qf[...], g, state, ks)
+    m.attn[...] = attn
+    dqf = dots(dot_nt, [g.astype(BF16)], kv) * rden + dden * ks
+    xv = m.xv[...]
+    dq = dqf * slope(dot(xv, m.wqv[...]))
+    m.dq[...] = dq
+    put_slices(m.csrc, 0, dots(dot_tn, [xv], split(dq, 2)))
+
+    sum1.scatter()
     red2.along(1)
-    sum1.scatter()
-
     def add_piece(n, base):
         def one(i, carry):
             m.ysum[n, i] = (m.ysend[base + i].astype(F32) + m.ybuf[n, i].astype(F32)).astype(BF16)
@@ -474,7 +554,6 @@
 
         lax.fori_loop(0, blocks, one, 0)
 
-    red2.gather()
     f_above.wait_recv()
     f_below.wait_recv()
 
@@ -488,6 +567,42 @@
 
     s6 = go(25, m.xr.at[0, :, keep], m.xr.at[0, :, keep], sibling)
     s7 = go(26, m.xr.at[1, :, keep], m.xr.at[1, :, keep], sibling)
+    project(m.xo[: nown // 2], 0)
+    project(m.xo[nown // 2 :], nown // 2)
+    s6.wait_recv()
+    s7.wait_recv()
+    for side in range(2):
+        project(m.xr[side], nown + side * nb)
+    m.fprod[tiles] = jnp.zeros((size, w), F32)
+    m.xprod[tiles] = jnp.zeros((size, w), F32)
+
+    def fore_one(t, carry):
+        tile = m.adjv[t]
+        b = m.cols[t]
+        before = m.ords[2, t]
+        m.fprod[t] = dot(tile, m.ext[b]) + m.fprod[before]
+        m.xprod[t] = dot(tile, m.xp[b]) + m.xprod[before]
+        return carry
+
+    lax.fori_loop(0, tiles, fore_one, 0, unroll=tiles // 2)
+    graph = None
+    for b in range(blocks):
+        term = dots(dot_tn, split(m.xprod[m.ords[3, b]], 2), [m.g5[b]])
+        graph = term if graph is None else graph + term
+    put_slices(m.esrc, 0, graph)
+    sum2.scatter()
+    red2.gather()
+    mine = m.bst[f]
+    hstate = split(square(dots(dot, split(open_rows(mine[0:8]), 3), [fold])), 2)
+    hdk = (dots(dot_nt, [m.hval[...]], hstate) + mine[8:9]) * slope(m.hkey[...])
+    hdk = split(hdk, 2)
+    lane = lanes(w, 128)[1] // HD
+    total = jnp.zeros((w, 128), F32)
+    for b in range(blocks):
+        total = total + jnp.where(lane == b, dots(dot_tn, [part_rows(b)], hdk), 0.0)
+    packed = fold_rows(dots(dot, split(total, 3), [fold]), 4)
+    m.ksrc[...] = packed.reshape(m.ksrc.shape)
+    keys.scatter()
     y0.wait_recv()
     add_piece(0, yu * per)
     y4 = go(23, m.ysum.at[0], m.ybuf.at[4], up_y)
@@ -496,38 +611,13 @@
     y5 = go(24, m.ysum.at[1], m.ybuf.at[5], down_y)
     place_rims(y * per)
     place_rims(y * per + blocks)
-    project(m.xo[nown // 2 :], nown // 2)
-    s6.wait_recv()
-    s7.wait_recv()
-    for side in range(2):
-        project(m.xr[side], nown + side * nb)
-    m.fprod[tiles] = jnp.zeros((size, w), F32)
-    m.xprod[tiles] = jnp.zeros((size, w), F32)
-
-    def fore_one(t, carry):
-        tile = m.adjv[t]
-        b = m.cols[t]
-        before = m.ords[2, t]
-        m.fprod[t] = dot(tile, m.ext[b]) + m.fprod[before]
-        m.xprod[t] = dot(tile, m.xp[b]) + m.xprod[before]
-        return carry
-
-    lax.fori_loop(0, tiles, fore_one, 0, unroll=tiles // 2)
-    graph = None
-    for b in range(blocks):
-        term = dots(dot_tn, split(m.xprod[m.ords[3, b]], 2), [m.g5[b]])
-        graph = term if graph is None else graph + term
-    put_slices(m.esrc, 1, graph)
-
+    sum1.along(0)
+    keys.along(0)
     red2.arrive()
-    small, dks = state_load(m.bst)
-    ds = split(block_diag(small), 2)
+    state, dks = open_states(m.bst)
+    ds = split(state, 2)
     xv = m.xv[...]
     dk = (dots(dot_nt, [m.vf[...]], ds) + dks) * slope(dot(xv, m.wkv[...]))
-    put_slices(m.esrc, 0, dots(dot_tn, [xv], split(dk, 2)))
-    sum2.scatter()
-    sum1.along(0)
-
     for b in range(blocks):
         here = slice(b * size, (b + 1) * size)
         m.layerv[here, :] = (0.5 * m.attn[here, :] + 0.5 * m.fprod[m.ords[3, b]]).astype(BF16)
@@ -544,7 +634,7 @@
         total = term if total is None else total + term
 
     sum2.along(0)
-
+    keys.gather()
     for copy in (y2, y3, y4, y5):
         copy.wait_recv()
 
@@ -564,15 +654,18 @@
     total = total + dots(dot_nt, split(m.pg[...].reshape(blocks * size, w), 2), [m.wgv[...]])
     m.gfeatv[...] = total.astype(BF16)
     outs.append(pltpu.make_async_copy(m.gfeatv, m.gfeat, m.ls.at[10]))
-    outs[2].start()
+    outs[-1].start()
     sum2.gather()
     sum1.arrive()
+    keys.arrive()
+    outs.append(pltpu.make_async_copy(m.kout, m.g3, m.ls.at[13]))
+    outs[-1].start()
     outs.append(pltpu.make_async_copy(m.cout, m.g1, m.ls.at[11]))
-    outs[3].start()
+    outs[-1].start()
     sum2.arrive()
     outs.append(pltpu.make_async_copy(m.eout, m.g2, m.ls.at[12]))
-    outs[4].start()
-    for red in (red1, red2, sum1, sum2):
+    outs[-1].start()
+    for red in (red1, red2, cots, sum1, sum2, keys):
         red.finish()
     for copy in singles:
         copy.wait_send()
@@ -580,7 +673,7 @@
         copy.wait()
 
 
-def last_kernel(layer_i, gfeat_i, c1, c2, st, layer, gfeat, gq, gk, gv, gg):
+def last_kernel(layer_i, gfeat_i, c1, c2, c3, st, layer, gfeat, gq, gk, gv, gg):
     layer[...] = layer_i[...]
     gfeat[...] = gfeat_i[...]
     n = gq.shape[0]
@@ -591,10 +684,17 @@
         return jnp.concatenate([ref[index * count + s].astype(F32) for s in range(count)], 0)
 
     gq[...] = mat(c1, 0)
-    gk[...] = mat(c2, 0)
-    gg[...] = mat(c2, 1)
-    small, _ = state_load(st)
-    gv[...] = dots(dot, split(mat(c1, 1), 2), split(block_diag(small), 2))
+    gg[...] = mat(c2, 0)
+    state, _ = open_states(st)
+    gv[...] = dots(dot, split(mat(c1, 1), 2), split(state, 2))
+    fold = fold_ones()
+    lane = lanes(n, n)[1] // HD
+    total = jnp.zeros((n, n), F32)
+    for h in range(HEADS):
+        rows = jnp.concatenate([c3[p] for p in range(h, c3.shape[0], HEADS)], 0)
+        rows = dot(open_rows(rows), fold)
+        total = total + jnp.where(lane == h, jnp.concatenate([rows] * (n // 128), 1), 0.0)
+    gk[...] = total
 
 
 def shards(xn, zn, x, wq, wk, wv, wg, adj, rows, cols, lists, cot):
@@ -621,8 +721,9 @@
         ("layer", S((n, w), BF16)),
         ("gfeat", S((n, w), BF16)),
         ("g1", S((owners, part, w), BF16)),
-        ("g2", S((owners, part, w), BF16)),
-        ("st2", S((8, 8, w), F32)),
+        ("g2", S((owners, part // 2, w), F32)),
+        ("g3", S((owners, HD * HEADS // 4 // xn, 128), BF16)),
+        ("st2", S((HEADS, 9, 128), F32)),
     ]
     scratch = [
         ("xv", V((n, w), BF16)),
@@ -635,8 +736,11 @@
         ("layerv", V((n, w), BF16)),
         ("gfeatv", V((n, w), BF16)),
         ("cout", V((owners, part, w), BF16)),
-        ("eout", V((owners, part, w), BF16)),
-        ("bst", V((8, 8, w), F32)),
+        ("eout", V((owners, part // 2, w), F32)),
+        ("kout", V((owners, HD * HEADS // 4 // xn, 128), BF16)),
+        ("bst", V((HEADS, 9, 128), F32)),
+        ("hkey", V((yn * CORES * size, 128), F32)),
+        ("hval", V((yn * CORES * size, 128), BF16)),
         ("kf", V((n, w), BF16)),
         ("vf", V((n, w), BF16)),
         ("qf", V((n, w), BF16)),
@@ -660,15 +764,23 @@
         ("pg", V((blocks, size, w), F32)),
         ("attn", V((n, w), F32)),
         ("dq", V((n, w), F32)),
-        ("ast", V((8, 8, w), F32)),
+        ("ast", V((HEADS, 9, 128), F32)),
         ("ordv", V((8, 128), jnp.int32)),
         ("ords", pltpu.SMEM((8, 128), jnp.int32)),
-        ("ls", pltpu.SemaphoreType.DMA((13,))),
+        ("ls", pltpu.SemaphoreType.DMA((14,))),
         ("ss", pltpu.SemaphoreType.DMA((singles,))),
         ("rs", pltpu.SemaphoreType.DMA((singles,))),
     ]
-    scratch += state_scratch("a", xn, zn, yn, w) + state_scratch("b", xn, zn, yn, w)
-    scratch += grad_scratch("c", xn, zn, yn, 2 * w, w) + grad_scratch("e", xn, zn, yn, 2 * w, w)
+    feats, ring, planes = yn * CORES, zn - 1 + xn - 1, owners - 1
+    tile = (9, 128)
+    scratch += sum_scratch("a", HEADS, xn, zn, tile, F32, 2 * (feats - 1) + ring, third=True)
+    scratch += sum_scratch("b", 1, xn, zn, tile, F32, feats - 1 + ring, third=True)
+    scratch += sum_scratch("g", HEADS, xn, 1, (size, 128), BF16, feats - 1)
+    scratch += sum_scratch("c", owners, xn, zn, (part, w), BF16, 2 * planes + zn - 1)
+    scratch += sum_scratch("e", owners, xn, zn, (part // 2, w), F32, 2 * planes + zn - 1)
+    scratch += [(n + "_" if n == "kf" else n, v) for n, v in sum_scratch(
+        "k", xn, xn, zn, (HD * HEADS // 4 // xn, 128), F32, planes + ring
+    )]
     names = [name for name, _ in ins + outs + scratch]
     made = pl.pallas_call(
         functools.partial(layer_kernel, names, xn, zn, yn),
@@ -685,7 +797,7 @@
     return pl.pallas_call(
         last_kernel,
         out_shape=[S((n, w), BF16)] * 2 + [S((w, w), F32)] * 4,
-        in_specs=[VM] * 5,
+        in_specs=[VM] * 6,
         out_specs=[VM] * 6,
         compiler_params=pltpu.CompilerParams(vmem_limit_bytes=LIMIT),
         name="last",

time: 77.4 us -> 72.8 us (0.941)
  Pallas kernels: 76.6 us -> 72.1 us
    pallas_call x1, Pallas kernels: 74 us -> 69.1 us  [shards(): pl.pallas_call(functools.partial(layer_kernel, names, xn, zn, yn), out_sh...]
where the time goes in v4:
time: 72.8 us; the launch traced here: 72.7 us
  Pallas kernels  72.1 us (99%)
    pallas_call x1, Pallas kernels, shards(): pl.pallas_call(functools.partial(layer_kernel, names, xn, zn, yn), out_sh...  69.1 us
    pallas_call x1, Pallas kernels, shards(): pl.pallas_call(last_kernel, out_shape=[S((n, w), BF16)] * 2 + [S((w, w),...  3 us

profile of v4, /device:TPU:1, one launch (start us, length us, event | category | flops | bytes accessed | tf_op | source)
XLA Modules:
  0.0 72.7 jit_solution(15806119124020471343)
XLA Ops:
  0.6 69.1 %layer.1 = (bf16[512,256]{1,0:T(8,128)(2,1)}, bf16[512,256]{1,0:T(8,128)(2,1)}, bf16[32,16,256]{2,1,0:T(8,128)(2,1)}, f32[32,8,256]{2,1,0:T(8,128)}, bf16[32,16,128]{2,1,0:T(8,128)(2,1)}, /*index=5*/f32[8,9,128]{2,1,0:T(8,128)}) custom-call(s32[48]{0:T(128)} %refs_0_.1, s32[48]{0:T(128)} %refs_1_.1, s32[2,8]{1,0:T(2,128)} %bitcast.1, ...), custom_call_target="tpu_custom_call" | custom-call | tf_op jit(solution)/shard_map/layer/pallas_call | solution.py:785
  69.7 3.0 %last.1 = (bf16[512,256]{1,0:T(8,128)(2,1)}, bf16[512,256]{1,0:T(8,128)(2,1)}, f32[256,256]{1,0:T(8,128)}, f32[256,256]{1,0:T(8,128)}, f32[256,256]{1,0:T(8,128)}, /*index=5*/f32[256,256]{1,0:T(8,128)}) custom-call(bf16[512,256]{1,0:T(8,128)(2,1)} %get-tuple-element.12.layer_i, bf16[512,256]{1,0:T(8,128)(2,1)} %get-tuple-element.13.gfeat_i, ...), custom_call_target="tpu_custom_call" | custom-call | tf_op jit(solution)/shard_map/last/pallas_call | solution.py:797

commit v5 on v4

--- a/solution.py
+++ b/solution.py
@@ -589,7 +589,10 @@
     for b in range(blocks):
         term = dots(dot_tn, split(m.xprod[m.ords[3, b]], 2), [m.g5[b]])
         graph = term if graph is None else graph + term
-    put_slices(m.esrc, 0, graph)
+    per2 = m.esrc.shape[1] // 2
+    for i in range(w // per2):
+        here = graph[i * per2 : (i + 1) * per2]
+        m.esrc[i] = jnp.concatenate([here[:, :128], here[:, 128:]], 0).astype(BF16)
     sum2.scatter()
     red2.gather()
     mine = m.bst[f]
@@ -684,7 +687,10 @@
         return jnp.concatenate([ref[index * count + s].astype(F32) for s in range(count)], 0)
 
     gq[...] = mat(c1, 0)
-    gg[...] = mat(c2, 0)
+    per = c2.shape[1] // 2
+    for i in range(n // per):
+        here = c2[i].astype(F32)
+        gg[i * per : (i + 1) * per, :] = jnp.concatenate([here[:per], here[per:]], 1)
     state, _ = open_states(st)
     gv[...] = dots(dot, split(mat(c1, 1), 2), split(state, 2))
     fold = fold_ones()
@@ -721,7 +727,7 @@
         ("layer", S((n, w), BF16)),
         ("gfeat", S((n, w), BF16)),
         ("g1", S((owners, part, w), BF16)),
-        ("g2", S((owners, part // 2, w), F32)),
+        ("g2", S((owners, part, w // 2), BF16)),
         ("g3", S((owners, HD * HEADS // 4 // xn, 128), BF16)),
         ("st2", S((HEADS, 9, 128), F32)),
     ]
@@ -736,7 +742,7 @@
         ("layerv", V((n, w), BF16)),
         ("gfeatv", V((n, w), BF16)),
         ("cout", V((owners, part, w), BF16)),
-        ("eout", V((owners, part // 2, w), F32)),
+        ("eout", V((owners, part, w // 2), BF16)),
         ("kout", V((owners, HD * HEADS // 4 // xn, 128), BF16)),
         ("bst", V((HEADS, 9, 128), F32)),
         ("hkey", V((yn * CORES * size, 128), F32)),
@@ -777,7 +783,7 @@
     scratch += sum_scratch("b", 1, xn, zn, tile, F32, feats - 1 + ring, third=True)
     scratch += sum_scratch("g", HEADS, xn, 1, (size, 128), BF16, feats - 1)
     scratch += sum_scratch("c", owners, xn, zn, (part, w), BF16, 2 * planes + zn - 1)
-    scratch += sum_scratch("e", owners, xn, zn, (part // 2, w), F32, 2 * planes + zn - 1)
+    scratch += sum_scratch("e", owners, xn, zn, (part, w // 2), BF16, 2 * planes + zn - 1)
     scratch += [(n + "_" if n == "kf" else n, v) for n, v in sum_scratch(
         "k", xn, xn, zn, (HD * HEADS // 4 // xn, 128), F32, planes + ring
     )]

time: 72.8 us -> 72 us (0.989)
  Pallas kernels: 72.1 us -> 71.2 us
    pallas_call x1, Pallas kernels: 69.1 us -> 68.2 us  [shards(): pl.pallas_call(functools.partial(layer_kernel, names, xn, zn, yn), out_sh...]
where the time goes in v5:
time: 72 us; the launch traced here: 71.8 us
  Pallas kernels  71.2 us (99%)
    pallas_call x1, Pallas kernels, shards(): pl.pallas_call(functools.partial(layer_kernel, names, xn, zn, yn), out_sh...  68.2 us
    pallas_call x1, Pallas kernels, shards(): pl.pallas_call(last_kernel, out_shape=[S((n, w), BF16)] * 2 + [S((w, w),...  2.98 us

profile of v5, /device:TPU:1, one launch (start us, length us, event | category | flops | bytes accessed | tf_op | source)
XLA Modules:
  0.0 71.8 jit_solution(1142146398351773174)
XLA Ops:
  0.6 68.2 %layer.1 = (bf16[512,256]{1,0:T(8,128)(2,1)}, bf16[512,256]{1,0:T(8,128)(2,1)}, bf16[32,16,256]{2,1,0:T(8,128)(2,1)}, bf16[32,16,128]{2,1,0:T(8,128)(2,1)}, bf16...) custom-call(s32[48]{0:T(128)} %refs_0_.1, s32[48]{0:T(128)} %refs_1_.1, s32[2,8]{1,0:T(2,128)} %bitcast.1, ...), custom_call_target="tpu_custom_call" | custom-call | tf_op jit(solution)/shard_map/layer/pallas_call | solution.py:791
  68.8 3.0 %last.1 = (bf16[512,256]{1,0:T(8,128)(2,1)}, bf16[512,256]{1,0:T(8,128)(2,1)}, f32[256,256]{1,0:T(8,128)}, f32[256,256]{1,0:T(8,128)}, f32[256,256]{1,0:T(8,128)}, /*index=5*/f32[256,256]{1,0:T(8,128)}) custom-call(bf16[512,256]{1,0:T(8,128)(2,1)} %get-tuple-element.12.layer_i, bf16[512,256]{1,0:T(8,128)(2,1)} %get-tuple-element.13.gfeat_i, ...), custom_call_target="tpu_custom_call" | custom-call | tf_op jit(solution)/shard_map/last/pallas_call | solution.py:803
